TPU v7x, 256 devices: a whole 4x4x8 slice. The times are simulated.
256 devices in a mesh: frame: 128 (over z, y, x_lo, core), head: 2 (over x_hi).
Axes of the slice: x: 4 (x_hi: 2, x_lo: 2; x = x_hi * 2 + x_lo), y: 4, z: 8, core: 2. Of those that a mesh axis runs over, the one named last changes fastest.
Arguments:
- queries: bfloat16 [16384, 1536], P('frame', 'head'), may hold values from -6 to 6
- keys: bfloat16 [16384, 1536], P('frame', 'head'), may hold values from -6 to 6
- values: bfloat16 [16384, 1536], P('frame', 'head'), may hold values from -6 to 6
- w_out: bfloat16 [1536, 1536], P('head'), may hold values from -0.15625 to 0.15625
- grad_proj: bfloat16 [16384, 1536], P('frame', 'head'), may hold values from -24 to 24
- frame_levels: int32 [256], replicated, may hold values from 0 to 2, as said below
Outputs:
- proj: bfloat16 [16384, 1536], P('frame', 'head')
- d_queries: bfloat16 [16384, 1536], P('frame', 'head')
- d_keys: bfloat16 [16384, 1536], P('frame', 'head')
- d_values: bfloat16 [16384, 1536], P('frame', 'head')
- d_wout: bfloat16 [1536, 1536], P('head', 'frame')
Inputs may be any that keep to these rules, and one draw needn't show every extreme that they name: `frame_levels`: within each clip the levels never rise along its frames; the counts of frames at levels 0, 1 and 2 in a clip are one of 7 0 9, 7 2 7, 6 3 7, 6 4 6, 6 5 5, 6 7 3, 5 8 3, 5 9 2, 5 10 1.
All inputs are finite; a program needn't handle non-finite values.
Results may differ from a plain program's by a relative error of at most 0.012.
The roundings to bfloat16 on the way count: a program that leaves them out, or rounds other values in their place, can miss the bound.
Values may be sent and summed in bfloat16 or wider, within the bound.
A program may use at most 64 MiB of HBM per device.

v0:
```python
from functools import partial

import jax
import jax.numpy as jnp
from jax import lax
from jax.sharding import PartitionSpec as P

HEAD_DIM = 64
CLIP_BLOCKS = 8
FRAMES_CLIP = 16


def from_behind(shard, axis, by):
    peers = lax.axis_size(axis)
    pairs = [(i, i + by) for i in range(peers) if 0 <= i + by < peers]
    return lax.ppermute(shard, axis, pairs)


def contract(left, right, dims_left, dims_right):
    return lax.dot_general(
        left, right, (((dims_left,), (dims_right,)), ((), ())), preferred_element_type=jnp.float32
    )


def head_math(mask, scale, operands):
    query, key_rows, value_rows, grad_rows = operands
    scores = contract(query, key_rows, 1, 1) * scale
    masked = jnp.where(mask, scores, -1e30)
    peak = jnp.max(masked, axis=1, keepdims=True)
    peak = jnp.where(jnp.any(mask, axis=1, keepdims=True), peak, 0.0)
    expo = jnp.where(mask, jnp.exp(scores - peak), 0.0)
    total = jnp.sum(expo, axis=1, keepdims=True)
    weights = expo / jnp.where(total > 0.0, total, 1.0)
    weights_low = weights.astype(jnp.bfloat16)
    attended = contract(weights_low, value_rows, 1, 0).astype(jnp.bfloat16)
    delta = jnp.sum(
        grad_rows.astype(jnp.float32) * attended.astype(jnp.float32), axis=1, keepdims=True
    )
    dprob = contract(grad_rows, value_rows, 1, 1)
    dscore = (weights * (dprob - delta)).astype(jnp.bfloat16)
    dquery = contract(dscore, key_rows, 1, 0) * scale
    dkey = contract(dscore, query, 0, 0) * scale
    dvalue = contract(weights_low, grad_rows, 0, 0)
    return (attended, dquery, dkey, dvalue)


def split_heads(rows):
    return rows.reshape(rows.shape[0], rows.shape[1] // HEAD_DIM, HEAD_DIM).transpose(1, 0, 2)


def join_heads(stacked):
    return stacked.transpose(1, 0, 2).reshape(stacked.shape[1], stacked.shape[0] * HEAD_DIM)


def local(queries, keys, values, w_out, grad_proj, frame_levels):
    block_len = queries.shape[0]
    feature_count = queries.shape[1]
    behind_blocks = CLIP_BLOCKS - 1
    span = (CLIP_BLOCKS + 1) * block_len
    front = behind_blocks * block_len
    clip_slots = CLIP_BLOCKS * block_len
    scale = HEAD_DIM ** (-0.5)
    here = lax.axis_index("frame")
    full_grad = lax.all_gather(grad_proj, "head", axis=1, tiled=True)
    grad_attn = contract(full_grad, w_out, 1, 1).astype(jnp.bfloat16)
    own = (keys, values)
    earlier = []
    current = own
    for step in range(behind_blocks):
        current = from_behind((current[0], current[1]), "frame", 1)
        earlier.append(current)
    following = from_behind((own[0], own[1]), "frame", -1)
    window = earlier[::-1] + [own, following]
    key_rows = jnp.concatenate([piece[0] for piece in window], axis=0)
    value_rows = jnp.concatenate([piece[1] for piece in window], axis=0)
    sizes = jnp.where(
        frame_levels == 0, block_len, jnp.where(frame_levels == 1, block_len // 4, block_len // 16)
    ).astype(jnp.int32)
    table = sizes.reshape(frame_levels.shape[0] // FRAMES_CLIP, FRAMES_CLIP)
    ends = jnp.cumsum(table, axis=1)
    starts = ends - table
    clip_here = here // CLIP_BLOCKS
    picked = jnp.arange(table.shape[0], dtype=jnp.int32) == clip_here
    start_row = jnp.sum(jnp.where(picked[:, None], starts, 0), axis=0)
    clip_total = jnp.sum(jnp.where(picked, ends[:, -1], 0))
    first_slot = here * block_len - clip_here * clip_slots
    query_off = first_slot + jnp.arange(block_len, dtype=jnp.int32)
    key_off = first_slot - front + jnp.arange(span, dtype=jnp.int32)
    live_query = query_off < clip_total
    live_key = (key_off >= 0) & (key_off < clip_total)
    frame_query = jnp.sum((start_row[None, :] <= query_off[:, None]).astype(jnp.int32), axis=1)
    frame_key = jnp.sum((start_row[None, :] <= key_off[:, None]).astype(jnp.int32), axis=1)
    mask = live_query[:, None] & live_key[None, :] & (frame_key[None, :] <= frame_query[:, None])
    attended, dquery, dkey, dvalue = lax.map(
        partial(head_math, mask, scale),
        (
            split_heads(queries),
            split_heads(key_rows),
            split_heads(value_rows),
            split_heads(grad_attn),
        ),
    )
    attn = join_heads(attended)
    d_queries = join_heads(dquery).astype(jnp.bfloat16)
    dkey_win = join_heads(dkey)
    dvalue_win = join_heads(dvalue)
    key_parts = [
        dkey_win[index * block_len : (index + 1) * block_len] for index in range(CLIP_BLOCKS + 1)
    ]
    value_parts = [
        dvalue_win[index * block_len : (index + 1) * block_len] for index in range(CLIP_BLOCKS + 1)
    ]
    from_before = (
        from_behind(key_parts[CLIP_BLOCKS].astype(jnp.bfloat16), "frame", 1).astype(jnp.float32),
        from_behind(value_parts[CLIP_BLOCKS].astype(jnp.bfloat16), "frame", 1).astype(jnp.float32),
    )
    carried = (
        jnp.zeros((block_len, feature_count), jnp.float32),
        jnp.zeros((block_len, feature_count), jnp.float32),
    )
    for dist in range(behind_blocks, 0, -1):
        carried = (
            carried[0] + key_parts[behind_blocks - dist],
            carried[1] + value_parts[behind_blocks - dist],
        )
        carried = from_behind((carried[0], carried[1]), "frame", -1)
    d_keys = (key_parts[behind_blocks] + from_before[0] + carried[0]).astype(jnp.bfloat16)
    d_values = (value_parts[behind_blocks] + from_before[1] + carried[1]).astype(jnp.bfloat16)
    partial_proj = jnp.dot(attn, w_out, preferred_element_type=jnp.float32)
    proj = lax.psum_scatter(
        partial_proj.astype(jnp.bfloat16), "head", scatter_dimension=1, tiled=True
    )
    weight_term = contract(attn, full_grad, 0, 0)
    d_wout = lax.psum_scatter(weight_term, "frame", scatter_dimension=1, tiled=True).astype(
        jnp.bfloat16
    )
    return (proj, d_queries, d_keys, d_values, d_wout)


def solution(mesh):
    in_specs = (
        P("frame", "head"),
        P("frame", "head"),
        P("frame", "head"),
        P("head", None),
        P("frame", "head"),
        P(),
    )
    out_specs = (
        P("frame", "head"),
        P("frame", "head"),
        P("frame", "head"),
        P("frame", "head"),
        P("head", "frame"),
    )
    return jax.shard_map(local, mesh=mesh, in_specs=in_specs, out_specs=out_specs, check_vma=False)
```

profile of v0, /device:TPU:1, one launch (start us, length us, event | category | flops | bytes accessed | tf_op | source)
XLA Modules:
  0.0 821.6 jit_solution(9822811469668559292)
XLA Ops:
  8.5 4.5 collective-permute-start
  22.5 9.7 %all_gather.3 = bf16[128,1536]{1,0:T(8,128)(2,1)S(1)} all-gather(bf16[128,768]{1,0:T(8,128)(2,1)} %param.12), channel_id=1, replica_groups=mesh['frame'=128,'head'=2] {'head'}, dimensions={1}, use_global_device_ids=true | all-gather | bytes 589824 | tf_op jit(solution)/shard_map/all_gather | solution.py:64
  33.1 4.6 collective-permute-start.1
  41.4 4.0 collective-permute-start.2
  48.6 4.0 collective-permute-start.3
  55.6 4.4 collective-permute-start.4
  60.1 3.3 collective-permute-start.12
  63.4 4.5 collective-permute-start.5
  68.6 3.3 collective-permute-start.13
  71.9 4.5 collective-permute-start.6
  88.8 118.4 %while.18 = (s32[]{:T(128)}, bf16[12,128,64]{1,2,0:T(8,128)(2,1)S(1)}, bf16[12,128,64]{1,2,0:T(8,128)(2,1)}, f32[12,1152,64]{1,2,0:T(8,128)}, f32[12,1152,64]{1,...) while((s32[]{:T(128)}, ...), condition=%wide.region_10.11_spmd.clone, body=%wide.region_6.10_spmd.clone.sunk | while | flops 116760576 | bytes 6393105 | solution.py:94
  207.1 3.2 fusion.40
  215.4 4.8 collective-permute-done.25
  254.8 376.0 %fusion.2 = f32[768,16]{0,1:T(8,128)} fusion(f32[768,1536]{0,1:T(8,128)} %fusion.43), kind=kCustom, calls=%all-reduce-scatter | all-reduce-scatter fusion | flops 1572865 | bytes 4768768
  647.2 7.0 collective-permute-start.38
  654.3 13.0 %collective-permute-start.39 = (bf16[768,16]{0,1:T(8,128)(2,1)}, bf16[768,16]{0,1:T(8,128)(2,1)}, u32[]{:S(2)}, u32[]{:S(2)}) collective-permute-start(bf16[768,16]{0,1:T(8,128)(2,1)} %convert.79), channel_id=1, source_target_pairs={{0,16},{2,18},{4,20},{6,22},{8,24},{10,26},{12,28},{14,30},{16,32}... | collective-permute-start | bytes 73736
  672.9 9.3 %collective-permute-start.42 = (bf16[768,16]{0,1:T(8,128)(2,1)}, bf16[768,16]{0,1:T(8,128)(2,1)}, u32[]{:S(2)}, u32[]{:S(2)}) collective-permute-start(bf16[768,16]{0,1:T(8,128)(2,1)} %convert.79), channel_id=1, source_target_pairs={{0,22},{2,24},{4,26},{6,28},{8,30},{10,32},{12,34},{14,36},{16,38}... | collective-permute-start | bytes 73736
  686.1 5.1 collective-permute-start.45
  698.7 3.1 collective-permute-start.49
  713.3 5.1 collective-permute-start.53
  723.9 3.4 collective-permute-start.54
  747.5 3.9 collective-permute-start.61
  751.4 3.4 collective-permute-start.62
  762.3 47.3 %concatenate.8 = bf16[768,524]{0,1:T(8,128)(2,1)} concatenate(bf16[768,12]{0,1:T(8,128)(2,1)} %copy-done.10, bf16[768,16]{0,1:T(8,128)(2,1)S(1)} %collective-permute-done.62, bf16[768,16]{0,1:T(8,128)(2,1)S(1)} %collective-permute-done.61, bf16[768,16]{0,1:T(8,128)(2,1)} %copy-done.25, bf16[768,16]{0,1:T(8,128)(2,1)} %copy-done.24, bf16[768,16]{0,1:T(8,128)(2,1)} %copy-done.23, ...), dimensions={1} | concatenate | bytes 1634304
  (367 shorter events, 274.3 us)
Async XLA Ops:
  7.2 807.6 %reduce-scatter.4.cloned.1.call-start = ((), (), s32[]{:S(2)}) async-start(), calls=%async_computation.1 | async-start | bytes 589824 | tf_op jit(solution)/shard_map/reduce_scatter | solution.py:130
  8.5 24.6 %collective-permute-start = (bf16[128,768]{0,1:T(8,128)(2,1)S(1)}, bf16[128,768]{0,1:T(8,128)(2,1)}, u32[]{:S(2)}, u32[]{:S(2)}) collective-permute-start(bf16[128,768]{0,1:T(8,128)(2,1)S(1)} %copy.60), channel_id=1, source_target_pairs={{0,2},{2,4},{4,6},{6,8},{8,10},{10,12},{12,14},{14,16},{16,18},{18... | collective-permute-start | bytes 589832 | tf_op jit(solution)/shard_map/ppermute | solution.py:16
  13.0 72.3 %collective-permute-start.7 = (bf16[128,768]{0,1:T(8,128)(2,1)S(1)}, bf16[128,768]{0,1:T(8,128)(2,1)}, u32[]{:S(2)}, u32[]{:S(2)}) collective-permute-start(bf16[128,768]{0,1:T(8,128)(2,1)S(1)} %copy.60), channel_id=1, source_target_pairs={{2,0},{4,2},{6,4},{8,6},{10,8},{12,10},{14,12},{16,14},{18,16},{20... | collective-permute-start | bytes 589832 | tf_op jit(solution)/shard_map/ppermute | solution.py:16
  17.3 22.1 %collective-permute-start.8 = (bf16[128,768]{0,1:T(8,128)(2,1)}, bf16[128,768]{0,1:T(8,128)(2,1)}, u32[]{:S(2)}, u32[]{:S(2)}) collective-permute-start(bf16[128,768]{0,1:T(8,128)(2,1)} %copy.63), channel_id=1, source_target_pairs={{0,2},{2,4},{4,6},{6,8},{8,10},{10,12},{12,14},{14,16},{16,18},{18... | collective-permute-start | bytes 589832 | tf_op jit(solution)/shard_map/ppermute | solution.py:16
  20.4 65.9 %collective-permute-start.15 = (bf16[128,768]{0,1:T(8,128)(2,1)}, bf16[128,768]{0,1:T(8,128)(2,1)}, u32[]{:S(2)}, u32[]{:S(2)}) collective-permute-start(bf16[128,768]{0,1:T(8,128)(2,1)} %copy.63), channel_id=1, source_target_pairs={{2,0},{4,2},{6,4},{8,6},{10,8},{12,10},{14,12},{16,14},{18,16},{20... | collective-permute-start | bytes 589832 | tf_op jit(solution)/shard_map/ppermute | solution.py:16
  248.6 442.7 %collective-permute-start.29 = (f32[128,768]{0,1:T(8,128)}, f32[128,768]{0,1:T(8,128)}, u32[]{:S(2)}, u32[]{:S(2)}) collective-permute-start(f32[128,768]{0,1:T(8,128)} %bitcast_add_fusion.2), channel_id=1, source_target_pairs={{2,0},{4,2},{6,4},{8,6},{10,8},{12,10},{14,12},{16,14},{18,16},{20... | collective-permute-start | bytes 1179656 | tf_op jit(solution)/shard_map/ppermute | solution.py:16
  252.7 450.9 %collective-permute-start.21 = (f32[128,768]{0,1:T(8,128)}, f32[128,768]{0,1:T(8,128)}, u32[]{:S(2)}, u32[]{:S(2)}) collective-permute-start(f32[128,768]{0,1:T(8,128)} %bitcast_add_fusion.9), channel_id=1, source_target_pairs={{2,0},{4,2},{6,4},{8,6},{10,8},{12,10},{14,12},{16,14},{18,16},{20... | collective-permute-start | bytes 1179656 | tf_op jit(solution)/shard_map/ppermute | solution.py:16
  645.3 21.9 %collective-permute-start.37 = (bf16[768,16]{0,1:T(8,128)(2,1)}, bf16[768,16]{0,1:T(8,128)(2,1)}, u32[]{:S(2)}, u32[]{:S(2)}) collective-permute-start(bf16[768,16]{0,1:T(8,128)(2,1)} %convert.79), channel_id=1, source_target_pairs={{0,12},{2,14},{4,16},{6,18},{8,20},{10,22},{12,24},{14,26},{16,28}... | collective-permute-start | bytes 73736
  647.2 22.9 %collective-permute-start.38 = (bf16[768,16]{0,1:T(8,128)(2,1)}, bf16[768,16]{0,1:T(8,128)(2,1)}, u32[]{:S(2)}, u32[]{:S(2)}) collective-permute-start(bf16[768,16]{0,1:T(8,128)(2,1)} %convert.79), channel_id=1, source_target_pairs={{0,14},{2,16},{4,18},{6,20},{8,22},{10,24},{12,26},{14,28},{16,30}... | collective-permute-start | bytes 73736
  654.3 18.6 %collective-permute-start.39 = (bf16[768,16]{0,1:T(8,128)(2,1)}, bf16[768,16]{0,1:T(8,128)(2,1)}, u32[]{:S(2)}, u32[]{:S(2)}) collective-permute-start(bf16[768,16]{0,1:T(8,128)(2,1)} %convert.79), channel_id=1, source_target_pairs={{0,16},{2,18},{4,20},{6,22},{8,24},{10,26},{12,28},{14,30},{16,32}... | collective-permute-start | bytes 73736
  667.2 15.0 %collective-permute-start.40 = (bf16[768,16]{0,1:T(8,128)(2,1)}, bf16[768,16]{0,1:T(8,128)(2,1)}, u32[]{:S(2)}, u32[]{:S(2)}) collective-permute-start(bf16[768,16]{0,1:T(8,128)(2,1)} %convert.79), channel_id=1, source_target_pairs={{0,18},{2,20},{4,22},{6,24},{8,26},{10,28},{12,30},{14,32},{16,34}... | collective-permute-start | bytes 73736
  696.1 14.1 %collective-permute-start.48 = (bf16[768,16]{0,1:T(8,128)(2,1)}, bf16[768,16]{0,1:T(8,128)(2,1)S(1)}, u32[]{:S(2)}, u32[]{:S(2)}) collective-permute-start(bf16[768,16]{0,1:T(8,128)(2,1)} %convert.79), channel_id=1, source_target_pairs={{0,34},{2,36},{4,38},{6,40},{8,42},{10,44},{12,46},{14,48},{16,50}... | collective-permute-start | bytes 73736
  698.7 14.6 %collective-permute-start.49 = (bf16[768,16]{0,1:T(8,128)(2,1)}, bf16[768,16]{0,1:T(8,128)(2,1)S(1)}, u32[]{:S(2)}, u32[]{:S(2)}) collective-permute-start(bf16[768,16]{0,1:T(8,128)(2,1)} %convert.79), channel_id=1, source_target_pairs={{0,36},{2,38},{4,40},{6,42},{8,44},{10,46},{12,48},{14,50},{16,52}... | collective-permute-start | bytes 73736
  701.9 16.5 %collective-permute-start.50 = (bf16[768,16]{0,1:T(8,128)(2,1)}, bf16[768,16]{0,1:T(8,128)(2,1)S(1)}, u32[]{:S(2)}, u32[]{:S(2)}) collective-permute-start(bf16[768,16]{0,1:T(8,128)(2,1)} %convert.79), channel_id=1, source_target_pairs={{0,38},{2,40},{4,42},{6,44},{8,46},{10,48},{12,50},{14,52},{16,54}... | collective-permute-start | bytes 73736
  703.7 26.3 %collective-permute-start.30 = (f32[128,768]{0,1:T(8,128)}, f32[128,768]{0,1:T(8,128)}, u32[]{:S(2)}, u32[]{:S(2)}) collective-permute-start(f32[128,768]{0,1:T(8,128)} %bitcast_add_fusion.1), channel_id=1, source_target_pairs={{2,0},{4,2},{6,4},{8,6},{10,8},{12,10},{14,12},{16,14},{18,16},{20... | collective-permute-start | bytes 1179656 | tf_op jit(solution)/shard_map/ppermute | solution.py:16
  707.9 16.0 %collective-permute-start.51 = (bf16[768,16]{0,1:T(8,128)(2,1)}, bf16[768,16]{0,1:T(8,128)(2,1)}, u32[]{:S(2)}, u32[]{:S(2)}) collective-permute-start(bf16[768,16]{0,1:T(8,128)(2,1)} %convert.79), channel_id=1, source_target_pairs={{0,40},{2,42},{4,44},{6,46},{8,48},{10,50},{12,52},{14,54},{16,56}... | collective-permute-start | bytes 73736
  710.3 17.1 %collective-permute-start.52 = (bf16[768,16]{0,1:T(8,128)(2,1)}, bf16[768,16]{0,1:T(8,128)(2,1)}, u32[]{:S(2)}, u32[]{:S(2)}) collective-permute-start(bf16[768,16]{0,1:T(8,128)(2,1)} %convert.79), channel_id=1, source_target_pairs={{0,42},{2,44},{4,46},{6,48},{8,50},{10,52},{12,54},{14,56},{16,58}... | collective-permute-start | bytes 73736
  713.3 15.4 %collective-permute-start.53 = (bf16[768,16]{0,1:T(8,128)(2,1)}, bf16[768,16]{0,1:T(8,128)(2,1)}, u32[]{:S(2)}, u32[]{:S(2)}) collective-permute-start(bf16[768,16]{0,1:T(8,128)(2,1)} %convert.79), channel_id=1, source_target_pairs={{0,44},{2,46},{4,48},{6,50},{8,52},{10,54},{12,56},{14,58},{16,60}... | collective-permute-start | bytes 73736
  719.0 21.7 %collective-permute-start.22 = (f32[128,768]{0,1:T(8,128)}, f32[128,768]{0,1:T(8,128)}, u32[]{:S(2)}, u32[]{:S(2)}) collective-permute-start(f32[128,768]{0,1:T(8,128)} %bitcast_add_fusion.8), channel_id=1, source_target_pairs={{2,0},{4,2},{6,4},{8,6},{10,8},{12,10},{14,12},{16,14},{18,16},{20... | collective-permute-start | bytes 1179656 | tf_op jit(solution)/shard_map/ppermute | solution.py:16
  736.4 15.0 %collective-permute-start.60 = (bf16[768,16]{0,1:T(8,128)(2,1)}, bf16[768,16]{0,1:T(8,128)(2,1)S(1)}, u32[]{:S(2)}, u32[]{:S(2)}) collective-permute-start(bf16[768,16]{0,1:T(8,128)(2,1)} %convert.79), channel_id=1, source_target_pairs={{0,58},{2,60},{4,62},{6,64},{8,66},{10,68},{12,70},{14,72},{16,74}... | collective-permute-start | bytes 73736
  737.7 73.2 %collective-permute-start.31 = (f32[128,768]{0,1:T(8,128)}, f32[128,768]{0,1:T(8,128)}, u32[]{:S(2)}, u32[]{:S(2)}) collective-permute-start(f32[128,768]{0,1:T(8,128)} %bitcast_add_fusion), channel_id=1, source_target_pairs={{2,0},{4,2},{6,4},{8,6},{10,8},{12,10},{14,12},{16,14},{18,16},{20... | collective-permute-start | bytes 1179656 | tf_op jit(solution)/shard_map/ppermute | solution.py:16
  740.7 70.3 %collective-permute-start.24 = (bf16[128,768]{0,1:T(8,128)(2,1)}, bf16[128,768]{0,1:T(8,128)(2,1)}, u32[]{:S(2)}, u32[]{:S(2)}) collective-permute-start(bf16[128,768]{0,1:T(8,128)(2,1)} %bitcast.161), channel_id=1, source_target_pairs={{0,2},{2,4},{4,6},{6,8},{8,10},{10,12},{12,14},{14,16},{16,18},{18... | collective-permute-start | bytes 589832 | tf_op jit(solution)/shard_map/ppermute | solution.py:16
  745.1 67.7 %collective-permute-start.23 = (f32[128,768]{0,1:T(8,128)}, f32[128,768]{0,1:T(8,128)}, u32[]{:S(2)}, u32[]{:S(2)}) collective-permute-start(f32[128,768]{0,1:T(8,128)} %bitcast_add_fusion.7), channel_id=1, source_target_pairs={{2,0},{4,2},{6,4},{8,6},{10,8},{12,10},{14,12},{16,14},{18,16},{20... | collective-permute-start | bytes 1179656 | tf_op jit(solution)/shard_map/ppermute | solution.py:16
  759.5 53.3 %collective-permute-start.16 = (bf16[128,768]{0,1:T(8,128)(2,1)}, bf16[128,768]{0,1:T(8,128)(2,1)S(1)}, u32[]{:S(2)}, u32[]{:S(2)}) collective-permute-start(bf16[128,768]{0,1:T(8,128)(2,1)} %bitcast.14), channel_id=1, source_target_pairs={{0,2},{2,4},{4,6},{6,8},{8,10},{10,12},{12,14},{14,16},{16,18},{18... | collective-permute-start | bytes 589832 | tf_op jit(solution)/shard_map/ppermute | solution.py:16
  (69 other events, 1178.1 us)
Sparse Core Ops, SparseCore 0:
  724.0 14.9 reduce-scatter.3
where the time goes:
time: 829 us; the launch traced here: 822 us
  blocking collectives  386 us (47%)
  starting transfers between devices  185 us (22%)
  matrix products  91.7 us (11%)
  local copies, waits for them, and re-layouts  74.9 us (9%)
  other arithmetic  47.5 us (6%)
  waiting for transfers between devices  20.2 us (2%)
  between operations  15.8 us (2%)
    unnamed x1, blocking collectives  376 us
    unnamed x32, starting transfers between devices  96.4 us
    dot_general x74, matrix products, contract(): lax.dot_general(left, right, (((dims_left,), (dims_right,)), ((), ())), p...  90.4 us
    ppermute x32, starting transfers between devices, from_behind(): return lax.ppermute(shard, axis, pairs)  89 us
    unnamed x81, local copies, waits for them, and re-layouts  63.1 us
    ppermute x32, waiting for transfers between devices, from_behind(): return lax.ppermute(shard, axis, pairs)  19.2 us
  transfers between devices with their start and end apart: 65, of which 9 were waited for; matrix products, arithmetic and copies ran while one was open for 56% of the time, Pallas kernels for 0%

commit v1 on v0

v1 whole, which is shorter than its diff:
```python
import functools
import math

import jax
import jax.numpy as jnp
from jax import lax
from jax.experimental import pallas as pl
from jax.experimental.pallas import tpu as pltpu
from jax.sharding import PartitionSpec as P

MESH = pl.DeviceIdType.MESH
BF = jnp.bfloat16
F32 = jnp.float32
HD = 64
BLK = 128
QB = 256
SLOTS = 1024
FEAT = 768
WIDTH = 1536
FRAMES_CLIP = 16
EXP_SCALE = HD ** (-0.5) * math.log2(math.e)


def mm(left, right, dl, dr):
    return lax.dot_general(left, right, (((dl,), (dr,)), ((), ())), preferred_element_type=F32)


def lanes(block):
    return pl.ds(pl.multiple_of(block * BLK, BLK), BLK)


def kernel(
    q_ref, k_ref, v_ref, w_ref, g_ref, lev_ref,
    proj_ref, dq_ref, dk_ref, dv_ref, dw_ref,
    xt, rx, dat, rd, gfull, gt, gy, nat, lim_ref, prob, low, dsb,
    ot, att, attn, pown, psend, precv, acc, xc, dqkv, dkvc, rout,
    ay, dfull, zs, rz, fin, rf,
    s_x, s_xf, r_xa, r_xc, s_d, s_df, r_da, r_dc, s_g, r_g, s_gy, r_gy,
    s_at, s_atc, r_at, s_ay, r_ay, s_p, r_p, s_xc, r_xc2, s_o, s_oq, s_okv, r_o, r_oq,
    s_z, r_z, s_f, r_f,
):
    me = lax.axis_index("frame")
    hd = lax.axis_index("head")
    c = me % 2
    xl = (me // 2) % 2
    y = (me // 4) % 4
    z = me // 16
    s = me % 8
    clip8 = me - s
    j = s // 2
    sib = me + 1 - 2 * c
    pos = y * 2 + c
    others = (3 - j, j + 1 - 2 * (j % 2), (j + 2) % 4)

    def rcopy(src, dst, ss, rs, dev, head=hd):
        return pltpu.make_async_remote_copy(
            src_ref=src, dst_ref=dst, send_sem=ss, recv_sem=rs,
            device_id=(dev, head), device_id_type=MESH,
        )

    def lcopy(src, dst, sem):
        return pltpu.make_async_copy(src, dst, sem)

    def ydev(p):
        return z * 16 + (p // 2) * 4 + xl * 2 + p % 2

    def zdev(zz):
        return zz * 16 + me % 16

    bar = pltpu.get_barrier_semaphore()
    for d in range(1, 8):
        pl.semaphore_signal(bar, inc=1, device_id=(clip8 + (s + d) % 8, hd), device_id_type=MESH)
        pl.semaphore_signal(bar, inc=1, device_id=(zdev((z + d) % 8), hd), device_id_type=MESH)
    pl.semaphore_signal(bar, inc=1, device_id=(me, 1 - hd), device_id_type=MESH)
    yh = (y // 2) * 2
    for n in range(4):
        far = (yh + 2) % 4 + n // 2
        pl.semaphore_signal(
            bar, inc=1, device_id=(z * 16 + far * 4 + xl * 2 + n % 2, hd), device_id_type=MESH
        )

    for i, ref in enumerate((q_ref, k_ref, v_ref)):
        for t in range(6):
            tile = ref[:, t * BLK:(t + 1) * BLK].T
            xt[2 * t, i] = tile[:HD]
            xt[2 * t + 1, i] = tile[HD:]
    pl.semaphore_wait(bar, 19)

    gsend = rcopy(g_ref, gfull.at[:, pl.ds(pl.multiple_of(hd * FEAT, BLK), FEAT)], s_g.at[0], r_g.at[0], me, 1 - hd)
    gsend.start()
    gown = lcopy(g_ref, gfull.at[:, pl.ds(pl.multiple_of(hd * FEAT, BLK), FEAT)], s_g.at[1])
    gown.start()

    def scatter_plan(src, dst, ss, ra, rc):
        remote = []
        for n, jj in enumerate(others):
            base = clip8 + jj * 2
            remote.append(rcopy(src.at[3 * jj], dst.at[0, ..., lanes(s)], ss.at[3 * n], ra.at[s], base))
            remote.append(rcopy(src.at[3 * jj + 1], dst.at[0, ..., lanes(s)], ss.at[3 * n + 1], ra.at[s], base + 1))
            remote.append(rcopy(src.at[3 * jj + 2], dst.at[1, ..., lanes(s)], ss.at[3 * n + 2], rc.at[s], base + c))
        remote.append(rcopy(src.at[3 * j + 1 - c], dst.at[0, ..., lanes(s)], ss.at[9], ra.at[s], sib))
        remote.append(rcopy(src.at[3 * j + 2], dst.at[1, ..., lanes(s)], ss.at[10], rc.at[s], sib))
        local = [
            lcopy(src.at[3 * j + c], dst.at[0, ..., lanes(s)], ra.at[s]),
            lcopy(src.at[3 * j + 2], dst.at[1, ..., lanes(s)], rc.at[s]),
        ]
        return remote, local

    def wait_own(src, dst, ra, rc):
        for b in range(8):
            lcopy(src.at[0], dst.at[0, ..., lanes(b)], ra.at[b]).wait()

    def forward_shared(src, dst, fs, rc):
        plan = []
        for n, jj in enumerate(others):
            b = jj * 2 + c
            lcopy(src.at[0], dst.at[1, ..., lanes(b)], rc.at[b]).wait()
            copy = rcopy(dst.at[1, ..., lanes(b)], dst.at[1, ..., lanes(b)], fs.at[n], rc.at[b], sib)
            copy.start()
            plan.append(copy)
        lcopy(src.at[0], dst.at[1, ..., lanes(s)], rc.at[s]).wait()
        return plan

    def wait_shared(src, dst, rc):
        for jj in range(4):
            b = jj * 2 + 1 - c
            lcopy(src.at[0], dst.at[1, ..., lanes(b)], rc.at[b]).wait()

    x_remote, x_local = scatter_plan(xt, rx, s_x, r_xa, r_xc)
    for copy in x_remote + x_local:
        copy.start()

    slot_iota = lax.broadcasted_iota(jnp.int32, (1, SLOTS), 1)
    seen = jnp.zeros((1, SLOTS), jnp.int32)
    start = jnp.int32(0)
    for f in range(FRAMES_CLIP):
        level = lev_ref[(me // 8) * FRAMES_CLIP + f]
        end = start + jnp.where(level == 0, BLK, jnp.where(level == 1, BLK // 4, BLK // 16))
        seen = jnp.where((slot_iota >= start) & (slot_iota < end), end, seen)
        start = end
    lim_ref[...] = seen

    gown.wait()
    gsend.wait_recv()
    for t in range(3):
        part = mm(w_ref[t * QB:(t + 1) * QB, :], gfull[...], 1, 1).astype(BF)
        for n in range(4):
            dat[4 * t + n] = part[n * HD:(n + 1) * HD]
    d_remote, d_local = scatter_plan(dat, rd, s_d, r_da, r_dc)
    for copy in d_remote + d_local:
        copy.start()

    for t in range(12):
        tile = gfull[:, t * BLK:(t + 1) * BLK].T
        for n in range(8):
            row = t * BLK + n * 16
            gt[row // 192, (row % 192) // 48, row % 48:row % 48 + 16, :] = tile[n * 16:(n + 1) * 16]
    gy_remote = []
    for m in range(1, 8):
        p = (pos + m) % 8
        gy_remote.append(rcopy(gt.at[:, p // 2], gy.at[:, :, lanes(pos)], s_gy.at[m], r_gy.at[pos], ydev(p)))
    gy_local = lcopy(gt.at[:, y], gy.at[:, :, lanes(pos)], r_gy.at[pos])

    x_fwd = forward_shared(xt, rx, s_xf, r_xc)
    for copy in gy_remote:
        copy.start()
    gy_local.start()
    wait_own(xt, rx, r_xa, r_xc)

    def naturals(slot):
        for i in range(2):
            nat[slot, i] = rx[slot, 1 + i].T

    naturals(0)

    def forward(n, slot):
        q0 = n * QB
        nk = min(2 * n + 3, 8)
        kl = nk * BLK
        qt = rx[slot, 0, :, q0:q0 + QB]
        lim = lim_ref[:, q0:q0 + QB]
        peak = jnp.full((8, QB), -1e30, F32)
        for kc in range(nk):
            rows = slice(kc * BLK, (kc + 1) * BLK)
            sc = mm(nat[slot, 0, rows, :], qt, 1, 0)
            if kc * BLK >= q0:
                key = lax.broadcasted_iota(jnp.int32, (BLK, QB), 0) + kc * BLK
                sc = jnp.where(key < lim, sc, -1e30)
            prob[slot, n, rows, :] = sc
            peak = jnp.maximum(peak, jnp.max(sc.reshape(BLK // 8, 8, QB), axis=0))
        peak = jnp.max(peak, axis=0, keepdims=True)
        total = jnp.zeros((8, QB), F32)
        for kc in range(nk):
            rows = slice(kc * BLK, (kc + 1) * BLK)
            ex = jnp.exp2((prob[slot, n, rows, :] - peak) * EXP_SCALE)
            prob[slot, n, rows, :] = ex
            total = total + jnp.sum(ex.reshape(BLK // 8, 8, QB), axis=0)
        total = jnp.sum(total, axis=0, keepdims=True)
        inv = jnp.where(lim > 0, 1.0 / total, 0.0)
        for kc in range(nk):
            rows = slice(kc * BLK, (kc + 1) * BLK)
            wt = prob[slot, n, rows, :] * inv
            prob[slot, n, rows, :] = wt
            low[slot, n, rows, :] = wt.astype(BF)
        ot[slot, :, q0:q0 + QB] = mm(rx[slot, 2, :, :kl], low[slot, n, :kl, :], 1, 0).astype(BF)

    def backward(n, slot):
        q0 = n * QB
        nk = min(2 * n + 3, 8)
        kl = nk * BLK
        qt = rx[slot, 0, :, q0:q0 + QB]
        da = rd[slot, :, q0:q0 + QB]
        delta = jnp.sum(
            da.astype(F32) * ot[slot, :, q0:q0 + QB].astype(F32), axis=0, keepdims=True
        )
        for kc in range(nk):
            rows = slice(kc * BLK, (kc + 1) * BLK)
            dp = mm(nat[slot, 1, rows, :], da, 1, 0)
            dsb[rows, :] = (prob[slot, n, rows, :] * (dp - delta)).astype(BF)
        dqkv[slot, 0, :, q0:q0 + QB] = (mm(rx[slot, 1, :, :kl], dsb[:kl, :], 1, 0) * HD ** (-0.5)).astype(BF)
        acc[slot, 0, :, :kl] += mm(qt, dsb[:kl, :], 1, 1)
        acc[slot, 1, :, :kl] += mm(da, low[slot, n, :kl, :], 1, 1)

    at_remote = []
    for m in range(1, 8):
        b = (s + m) % 8
        at_remote.append(rcopy(ot.at[0, :, lanes(b)], att.at[3 * j + c], s_at.at[m], r_at.at[3 * j + c], clip8 + b))
    at_local = lcopy(ot.at[0, :, lanes(s)], att.at[3 * j + c], r_at.at[3 * j + c])

    def shared_block(n):
        return (1 - c) * (n + 4 * (n // 2)) + c * (n + 2)

    def fwd_item(i, carry):
        slot = i // 4
        qb = jnp.where(i < 4, i, shared_block(2 * (i % 2)) // 2)

        @pl.when(i == 4)
        def _():
            for copy in at_remote:
                copy.start()
            at_local.start()
            wait_shared(xt, rx, r_xc)
            naturals(1)

        for n in range(4):
            @pl.when(qb == n)
            def _(n=n):
                forward(n, slot)

        return carry

    lax.fori_loop(0, 6, fwd_item, 0)

    def shared_send(src, dst, ss, rs, n, block, op):
        @pl.when(block == s)
        def _():
            if op == "start":
                lcopy(src, dst, rs).start()

        @pl.when(block != s)
        def _():
            copy = rcopy(src, dst, ss.at[n], rs, clip8 + block)
            copy.start() if op == "start" else copy.wait_send()

    def atc(op):
        for n in range(4):
            b = shared_block(n)
            shared_send(ot.at[1, :, lanes(b)], att.at[3 * j + 2], s_atc, r_at.at[3 * j + 2], n, b, op)

    atc("start")

    d_fwd = forward_shared(dat, rd, s_df, r_dc)
    wait_shared(dat, rd, r_dc)
    acc[...] = jnp.zeros_like(acc)

    half_there = pl.ds(pl.multiple_of((1 - c) * 512, BLK), 512)
    half_here = pl.ds(pl.multiple_of(c * 512, BLK), 512)
    xc_copy = rcopy(acc.at[1, :, :, half_there], xc, s_xc.at[0], r_xc2.at[0], sib)

    def oq(op):
        for n in range(4):
            b = shared_block(n)
            shared_send(dqkv.at[1, 0, :, lanes(b)], rout.at[3 * j + 2, 0], s_oq, r_oq.at[3 * j + 2], n, b, op)

    def bwd_item(i, carry):
        slot = jnp.where(i < 2, 1, 0)
        qb = jnp.where(i < 2, shared_block(2 * (i % 2)) // 2, i - 2)

        @pl.when(i == 2)
        def _():
            xc_copy.start()
            oq("start")
            wait_own(dat, rd, r_da, r_dc)

        for n in range(4):
            @pl.when(qb == n)
            def _(n=n):
                backward(n, slot)

        return carry

    lax.fori_loop(0, 2, bwd_item, 0)
    for h in range(12):
        lcopy(att.at[0], att.at[h], r_at.at[h]).wait()
    for t in range(6):
        tile = att[2 * t:2 * t + 2].reshape(BLK, BLK).T
        attn[t // 3, :, (t % 3) * BLK:(t % 3 + 1) * BLK] = tile
    ay_remote = []
    for m in range(1, 8):
        p = (pos + m) % 8
        ay_remote.append(
            rcopy(attn.at[p % 2], ay.at[pl.ds(pl.multiple_of(pos * BLK, BLK), BLK), :], s_ay.at[m], r_ay.at[pos], ydev(p))
        )
    ay_local = lcopy(attn.at[c], ay.at[pl.ds(pl.multiple_of(pos * BLK, BLK), BLK), :], r_ay.at[pos])
    for copy in ay_remote:
        copy.start()
    ay_local.start()

    def project(half):
        cols = pl.ds(pl.multiple_of(half * FEAT, BLK), FEAT)
        return mm(attn[0], w_ref[:384, cols], 1, 0) + mm(attn[1], w_ref[384:, cols], 1, 0)

    psend[...] = project(1 - hd).astype(BF)
    p_copy = rcopy(psend, precv, s_p.at[0], r_p.at[0], me, 1 - hd)
    p_copy.start()
    pown[...] = project(hd)

    lax.fori_loop(2, 6, bwd_item, 0)
    for i in range(2):
        scale = HD ** (-0.5) if i == 0 else 1.0
        dqkv[0, 1 + i] = (acc[0, i] * scale).astype(BF)
    o_remote = []
    for m in range(1, 8):
        b = (s + m) % 8
        o_remote.append(rcopy(dqkv.at[0, :, :, lanes(b)], rout.at[3 * j + c], s_o.at[m], r_o.at[3 * j + c], clip8 + b))
    o_local = lcopy(dqkv.at[0, :, :, lanes(s)], rout.at[3 * j + c], r_o.at[3 * j + c])
    for copy in o_remote:
        copy.start()
    o_local.start()

    xc_copy.wait_recv()
    for i in range(2):
        scale = HD ** (-0.5) if i == 0 else 1.0
        dkvc[i] = ((acc[1, i, :, half_here] + xc[i]) * scale).astype(BF)

    def okv(op):
        for n in range(4):
            src = dkvc.at[:, :, n * BLK:(n + 1) * BLK]
            shared_send(src, rout.at[3 * j + 2, 1:3], s_okv, r_o.at[3 * j + 2], n, 4 * c + n, op)

    okv("start")

    for p in range(8):
        lcopy(gt.at[:, 0], gy.at[:, :, lanes(p)], r_gy.at[p]).wait()
        lcopy(attn.at[0], ay.at[p * BLK:(p + 1) * BLK, :], r_ay.at[p]).wait()
    for t in range(2):
        part = mm(gy[4 * t:4 * t + 4].reshape(192, SLOTS), ay[...], 1, 0)
        dfull[4 * t:4 * t + 4] = part.reshape(4, 48, 384)
    zs[...] = dfull[...].astype(BF)
    z_remote = []
    for m in range(1, 8):
        zz = (z + m) % 8
        z_remote.append(rcopy(zs.at[zz], rz.at[z], s_z.at[m], r_z.at[z], zdev(zz)))
    for copy in z_remote:
        copy.start()

    p_copy.wait_recv()
    proj_ref[...] = (pown[...] + precv[...].astype(F32)).astype(BF)

    for jj in range(4):
        for cc in range(2):
            lcopy(rout.at[0], rout.at[3 * jj + cc], r_o.at[3 * jj + cc]).wait()
        lcopy(rout.at[0, 0], rout.at[3 * jj + 2, 0], r_oq.at[3 * jj + 2]).wait()
        lcopy(rout.at[0, 1:3], rout.at[3 * jj + 2, 1:3], r_o.at[3 * jj + 2]).wait()
    for i, ref in enumerate((dq_ref, dk_ref, dv_ref)):
        for t in range(6):
            tile = rout[2 * t:2 * t + 2, i].reshape(BLK, BLK)
            ref[:, t * BLK:(t + 1) * BLK] = tile.T

    summed = dfull[z]
    for m in range(1, 8):
        zz = (z + m) % 8
        lcopy(zs.at[0], rz.at[zz], r_z.at[zz]).wait()
        summed = summed + rz[zz].astype(F32)
    fin[...] = summed.reshape(2, 24, 384)
    mine = xl * 2 + c
    f_remote = []
    for m in range(1, 4):
        t = (mine + m) % 4
        f_remote.append(
            rcopy(fin.at[t // 2], rf.at[mine], s_f.at[m], r_f.at[mine], me - mine + t)
        )
    for copy in f_remote:
        copy.start()
    rf[mine] = fin[xl]
    for m in range(1, 4):
        t = (mine + m) % 4
        lcopy(fin.at[0], rf.at[t], r_f.at[t]).wait()
    for cc in range(2):
        both = rf[cc] + rf[2 + cc]
        dw_ref[:, cc * 384:(cc + 1) * 384] = jnp.where(c == 0, both[:12], both[12:]).astype(BF)

    gsend.wait_send()
    for copy in x_remote + d_remote + x_fwd + d_fwd + gy_remote + at_remote + ay_remote + o_remote + z_remote + f_remote:
        copy.wait_send()
    xc_copy.wait_send()
    p_copy.wait_send()
    atc("wait")
    oq("wait")
    okv("wait")


def local(queries, keys, values, w_out, grad_proj, frame_levels):
    vmem = pl.BlockSpec(memory_space=pltpu.VMEM)
    smem = pl.BlockSpec(memory_space=pltpu.SMEM)
    rows = jax.ShapeDtypeStruct((BLK, FEAT), BF)
    dma = lambda n: pltpu.SemaphoreType.DMA((n,))
    scratch = [
        pltpu.VMEM((12, 3, HD, BLK), BF),
        pltpu.VMEM((2, 3, HD, SLOTS), BF),
        pltpu.VMEM((12, HD, BLK), BF),
        pltpu.VMEM((2, HD, SLOTS), BF),
        pltpu.VMEM((BLK, WIDTH), BF),
        pltpu.VMEM((8, 4, 48, BLK), BF),
        pltpu.VMEM((8, 48, SLOTS), BF),
        pltpu.VMEM((2, 2, SLOTS, HD), BF),
        pltpu.VMEM((1, SLOTS), jnp.int32),
        pltpu.VMEM((2, 4, SLOTS, QB), F32),
        pltpu.VMEM((2, 4, SLOTS, QB), BF),
        pltpu.VMEM((SLOTS, QB), BF),
        pltpu.VMEM((2, HD, SLOTS), BF),
        pltpu.VMEM((12, HD, BLK), BF),
        pltpu.VMEM((2, BLK, 384), BF),
        pltpu.VMEM((BLK, FEAT), F32),
        pltpu.VMEM((BLK, FEAT), BF),
        pltpu.VMEM((BLK, FEAT), BF),
        pltpu.VMEM((2, 2, HD, SLOTS), F32),
        pltpu.VMEM((2, HD, 512), F32),
        pltpu.VMEM((2, 3, HD, SLOTS), BF),
        pltpu.VMEM((2, HD, 512), BF),
        pltpu.VMEM((12, 3, HD, BLK), BF),
        pltpu.VMEM((SLOTS, 384), BF),
        pltpu.VMEM((8, 48, 384), F32),
        pltpu.VMEM((8, 48, 384), BF),
        pltpu.VMEM((8, 48, 384), BF),
        pltpu.VMEM((2, 24, 384), F32),
        pltpu.VMEM((4, 24, 384), F32),
    ] + [
        dma(n)
        for n in (
            11, 3, 8, 8, 11, 3, 8, 8, 2, 1, 8, 8,
            8, 4, 12, 8, 8, 1, 1, 1, 1, 8, 4, 4, 12, 12,
            8, 8, 4, 4,
        )
    ]
    proj, dq, dk, dv, dw = pl.pallas_call(
        kernel,
        out_shape=(rows, rows, rows, rows, jax.ShapeDtypeStruct((12, FEAT), BF)),
        in_specs=[vmem] * 5 + [smem],
        out_specs=[vmem] * 5,
        scratch_shapes=scratch,
        compiler_params=pltpu.CompilerParams(
            collective_id=0, has_side_effects=True, vmem_limit_bytes=56 * 1024 * 1024
        ),
    )(queries, keys, values, w_out, grad_proj, frame_levels)
    return proj, dq, dk, dv, dw.T


def solution(mesh):
    rows = P("frame", "head")
    return jax.shard_map(
        local,
        mesh=mesh,
        in_specs=(rows, rows, rows, P("head", None), rows, P()),
        out_specs=(rows, rows, rows, rows, P("head", "frame")),
        check_vma=False,
    )
```

time: 829 us -> 72 us (0.09)
  blocking collectives: 386 us -> 0 us
  starting transfers between devices: 185 us -> 0 us
  matrix products: 91.7 us -> 0 us
  local copies, waits for them, and re-layouts: 74.9 us -> 7.81 us
  Pallas kernels: 0 us -> 63.3 us
  other arithmetic: 47.5 us -> 0 us
  waiting for transfers between devices: 20.2 us -> 0 us
  between operations: 15.8 us -> 0.64 us
    unnamed x1 -> x0, blocking collectives: 376 us -> none
    unnamed x32 -> x0, starting transfers between devices: 96.4 us -> none
    dot_general x75 -> x0, matrix products: 91.7 us -> none  [the longest x74 90.4 us: contract(): lax.dot_general(left, right, (((dims_left,), (dims_right,)), ((), ())), p...]
    ppermute x32 -> x0, starting transfers between devices: 89 us -> none  [from_behind(): return lax.ppermute(shard, axis, pairs)]
    pallas_call x0 -> x1, Pallas kernels: none -> 63.3 us  [local(): pl.pallas_call(kernel, out_shape=(rows, rows, rows, rows, jax.ShapeDtypeS...]
    unnamed x81 -> x5, local copies, waits for them, and re-layouts: 63.1 us -> 7.81 us
    ppermute x32 -> x0, waiting for transfers between devices: 19.2 us -> none  [from_behind(): return lax.ppermute(shard, axis, pairs)]
    reduce_sum x28 -> x0, other arithmetic: 13.3 us -> none  [the longest x12 12 us: head_math(): total = jnp.sum(expo, axis=1, keepdims=True)]
  transfers between devices with their start and end apart: 65 -> 0, of which waited for: 9 -> 0; matrix products, arithmetic and copies ran while one was open for 56% -> 0% of each run, Pallas kernels for 0% -> 0%
where the time goes in v1:
time: 72 us; the launch traced here: 71.8 us
  Pallas kernels  63.3 us (88%)
  local copies, waits for them, and re-layouts  7.81 us (11%)
    pallas_call x1, Pallas kernels, local(): pl.pallas_call(kernel, out_shape=(rows, rows, rows, rows, jax.ShapeDtypeS...  63.3 us
    unnamed x5, local copies, waits for them, and re-layouts  7.81 us

profile of v1, /device:TPU:1, one launch (start us, length us, event | category | flops | bytes accessed | tf_op | source)
XLA Modules:
  0.0 71.8 jit_solution(5440982689208181676)
XLA Ops:
  0.6 63.3 %shard_map.101 = (bf16[128,768]{1,0:T(8,128)(2,1)}, bf16[128,768]{1,0:T(8,128)(2,1)}, bf16[128,768]{1,0:T(8,128)(2,1)}, bf16[128,768]{1,0:T(8,128)(2,1)}, bf16[12,768]{1,0:T(8,128)(2,1)}) custom-call(bf16[128,768]{1,0:T(8,128)(2,1)} %q_ref.1, bf16[128,768]{1,0:T(8,128)(2,1)} %k_ref.1, bf16[128,768]{1,0:T(8,128)(2,1)} %v_ref.1, bf16[768,1536]{1,0:T(8,128)(2,1)} %w_ref.1, ...), custom_call_target="tpu_custom_call" | custom-call | tf_op jit(solution)/shard_map/pallas_call | solution.py:456
  63.9 1.6 %copy.16 = bf16[128,768]{1,0:T(8,128)(2,1)} copy(bf16[128,768]{1,0:T(8,128)(2,1)} %get-tuple-element.20) | data formatting | bytes 393216
  65.6 1.6 %copy.17 = bf16[128,768]{1,0:T(8,128)(2,1)} copy(bf16[128,768]{1,0:T(8,128)(2,1)} %get-tuple-element.21) | data formatting | bytes 393216
  67.2 1.6 %copy.18 = bf16[128,768]{1,0:T(8,128)(2,1)} copy(bf16[128,768]{1,0:T(8,128)(2,1)} %get-tuple-element.22) | data formatting | bytes 393216
  68.8 1.6 %copy.19 = bf16[128,768]{1,0:T(8,128)(2,1)} copy(bf16[128,768]{1,0:T(8,128)(2,1)} %get-tuple-element.23) | data formatting | bytes 393216
  70.4 1.3 %copy.20 = bf16[768,12]{0,1:T(8,128)(2,1)} copy(bf16[768,12]{0,1:T(8,128)(2,1)} %bitcast.1) | data formatting | bytes 36864

commit v2 on v1

--- a/solution.py
+++ b/solution.py
@@ -30,11 +30,11 @@
 
 
 def kernel(
-    q_ref, k_ref, v_ref, w_ref, g_ref, lev_ref,
+    q_hbm, k_hbm, v_hbm, w_hbm, g_hbm, lev_ref,
     proj_ref, dq_ref, dk_ref, dv_ref, dw_ref,
-    xt, rx, dat, rd, gfull, gt, gy, nat, lim_ref, prob, low, dsb,
+    q_ref, k_ref, v_ref, w_ref, g_ref, s_in, xt, rx, dat, rd, gfull, gt, gy, nat, lim_ref, prob, low, dsb,
     ot, att, attn, pown, psend, precv, acc, xc, dqkv, dkvc, rout,
-    ay, dfull, zs, rz, fin, rf,
+    dpart, ay0, ay1, df0, df1, zs0, zs1, rz0, rz1, fin0, fin1, rf0, rf1,
     s_x, s_xf, r_xa, r_xc, s_d, s_df, r_da, r_dc, s_g, r_g, s_gy, r_gy,
     s_at, s_atc, r_at, s_ay, r_ay, s_p, r_p, s_xc, r_xc2, s_o, s_oq, s_okv, r_o, r_oq,
     s_z, r_z, s_f, r_f,
@@ -49,7 +49,9 @@
     clip8 = me - s
     j = s // 2
     sib = me + 1 - 2 * c
-    pos = y * 2 + c
+    far_y = 3 - y
+    group = y // 2
+    pos = group * 2 + c
     others = (3 - j, j + 1 - 2 * (j % 2), (j + 2) % 4)
 
     def rcopy(src, dst, ss, rs, dev, head=hd):
@@ -61,65 +63,68 @@
     def lcopy(src, dst, sem):
         return pltpu.make_async_copy(src, dst, sem)
 
-    def ydev(p):
-        return z * 16 + (p // 2) * 4 + xl * 2 + p % 2
+    def ydev(core):
+        return z * 16 + far_y * 4 + xl * 2 + core
 
     def zdev(zz):
         return zz * 16 + me % 16
+
+    loads = [
+        lcopy(src, dst, s_in.at[i])
+        for i, (src, dst) in enumerate(
+            ((q_hbm, q_ref), (k_hbm, k_ref), (v_hbm, v_ref), (g_hbm, g_ref), (w_hbm, w_ref))
+        )
+    ]
+    for copy in loads:
+        copy.start()
 
     bar = pltpu.get_barrier_semaphore()
     for d in range(1, 8):
         pl.semaphore_signal(bar, inc=1, device_id=(clip8 + (s + d) % 8, hd), device_id_type=MESH)
         pl.semaphore_signal(bar, inc=1, device_id=(zdev((z + d) % 8), hd), device_id_type=MESH)
     pl.semaphore_signal(bar, inc=1, device_id=(me, 1 - hd), device_id_type=MESH)
-    yh = (y // 2) * 2
-    for n in range(4):
-        far = (yh + 2) % 4 + n // 2
-        pl.semaphore_signal(
-            bar, inc=1, device_id=(z * 16 + far * 4 + xl * 2 + n % 2, hd), device_id_type=MESH
-        )
+    for core in range(2):
+        pl.semaphore_signal(bar, inc=1, device_id=(ydev(core), hd), device_id_type=MESH)
 
     for i, ref in enumerate((q_ref, k_ref, v_ref)):
+        loads[i].wait()
         for t in range(6):
             tile = ref[:, t * BLK:(t + 1) * BLK].T
             xt[2 * t, i] = tile[:HD]
             xt[2 * t + 1, i] = tile[HD:]
-    pl.semaphore_wait(bar, 19)
-
-    gsend = rcopy(g_ref, gfull.at[:, pl.ds(pl.multiple_of(hd * FEAT, BLK), FEAT)], s_g.at[0], r_g.at[0], me, 1 - hd)
-    gsend.start()
-    gown = lcopy(g_ref, gfull.at[:, pl.ds(pl.multiple_of(hd * FEAT, BLK), FEAT)], s_g.at[1])
-    gown.start()
+    pl.semaphore_wait(bar, 17)
 
     def scatter_plan(src, dst, ss, ra, rc):
         remote = []
+        shared = []
         for n, jj in enumerate(others):
             base = clip8 + jj * 2
             remote.append(rcopy(src.at[3 * jj], dst.at[0, ..., lanes(s)], ss.at[3 * n], ra.at[s], base))
             remote.append(rcopy(src.at[3 * jj + 1], dst.at[0, ..., lanes(s)], ss.at[3 * n + 1], ra.at[s], base + 1))
-            remote.append(rcopy(src.at[3 * jj + 2], dst.at[1, ..., lanes(s)], ss.at[3 * n + 2], rc.at[s], base + c))
+            shared.append(rcopy(src.at[3 * jj + 2], dst.at[1, ..., lanes(s)], ss.at[3 * n + 2], rc.at[s], base + c))
         remote.append(rcopy(src.at[3 * j + 1 - c], dst.at[0, ..., lanes(s)], ss.at[9], ra.at[s], sib))
-        remote.append(rcopy(src.at[3 * j + 2], dst.at[1, ..., lanes(s)], ss.at[10], rc.at[s], sib))
+        shared.append(rcopy(src.at[3 * j + 2], dst.at[1, ..., lanes(s)], ss.at[10], rc.at[s], sib))
         local = [
             lcopy(src.at[3 * j + c], dst.at[0, ..., lanes(s)], ra.at[s]),
             lcopy(src.at[3 * j + 2], dst.at[1, ..., lanes(s)], rc.at[s]),
         ]
-        return remote, local
+        return remote + shared, local
 
     def wait_own(src, dst, ra, rc):
         for b in range(8):
             lcopy(src.at[0], dst.at[0, ..., lanes(b)], ra.at[b]).wait()
 
+    def shared_plan(dst, fs, rc):
+        return [
+            rcopy(dst.at[1, ..., lanes(jj * 2 + c)], dst.at[1, ..., lanes(jj * 2 + c)], fs.at[n], rc.at[jj * 2 + c], sib)
+            for n, jj in enumerate(others)
+        ]
+
     def forward_shared(src, dst, fs, rc):
-        plan = []
-        for n, jj in enumerate(others):
-            b = jj * 2 + c
-            lcopy(src.at[0], dst.at[1, ..., lanes(b)], rc.at[b]).wait()
-            copy = rcopy(dst.at[1, ..., lanes(b)], dst.at[1, ..., lanes(b)], fs.at[n], rc.at[b], sib)
+        for copy, jj in zip(shared_plan(dst, fs, rc), others):
+            lcopy(src.at[0], dst.at[1, ..., lanes(jj * 2 + c)], rc.at[jj * 2 + c]).wait()
             copy.start()
-            plan.append(copy)
         lcopy(src.at[0], dst.at[1, ..., lanes(s)], rc.at[s]).wait()
-        return plan
 
     def wait_shared(src, dst, rc):
         for jj in range(4):
@@ -140,31 +145,51 @@
         start = end
     lim_ref[...] = seen
 
-    gown.wait()
-    gsend.wait_recv()
+    def transposed_half(half):
+        for t in range(6):
+            cols = pl.ds(pl.multiple_of(half * FEAT + t * BLK, BLK), BLK)
+            tile = gfull[:, cols].T
+            for n in range(8):
+                row = t * BLK + n * 16
+                gt[4 * half + row // 192, (row % 192) // 48, row % 48:row % 48 + 16, :] = tile[n * 16:(n + 1) * 16]
+
+    def gt_part(half, which_group):
+        return gt.at[pl.ds(4 * half, 4), pl.ds(2 * which_group, 2)]
+
+    def gy_part(half, p):
+        return gy.at[pl.ds(4 * half, 4), :, :, lanes(p)]
+
+    def gy_plan(half, which):
+        return [
+            rcopy(gt_part(half, 1 - group), gy_part(half, pos), s_gy.at[which, 0], r_gy.at[which, pos], ydev(c)),
+            rcopy(gt_part(half, group), gy_part(half, pos), s_gy.at[which, 1], r_gy.at[which, pos], sib),
+            lcopy(gt_part(half, group), gy_part(half, pos), r_gy.at[which, pos]),
+        ]
+
+    def gy_wait(half, which, p):
+        lcopy(gt_part(half, group), gy_part(half, p), r_gy.at[which, p]).wait()
+
+    def gy_forward(half, which):
+        p = (1 - group) * 2 + c
+        gy_wait(half, which, p)
+        copy = rcopy(gy_part(half, p), gy_part(half, p), s_gy.at[which, 2], r_gy.at[which, p], sib)
+        copy.start()
+        return [copy]
+
+    loads[3].wait()
+    own_cols = pl.ds(pl.multiple_of(hd * FEAT, BLK), FEAT)
+    gfull[:, own_cols] = g_ref[...]
+    transposed_half(hd)
+    loads[4].wait()
     for t in range(3):
-        part = mm(w_ref[t * QB:(t + 1) * QB, :], gfull[...], 1, 1).astype(BF)
-        for n in range(4):
-            dat[4 * t + n] = part[n * HD:(n + 1) * HD]
-    d_remote, d_local = scatter_plan(dat, rd, s_d, r_da, r_dc)
-    for copy in d_remote + d_local:
+        dpart[t * QB:(t + 1) * QB, :] = mm(w_ref[t * QB:(t + 1) * QB, own_cols], g_ref[...], 1, 1)
+    for copy in x_remote:
+        copy.wait_send()
+    gsend = rcopy(g_ref, gfull.at[:, own_cols], s_g.at[0], r_g.at[0], me, 1 - hd)
+    gsend.start()
+    gy_near = gy_plan(hd, 0)
+    for copy in gy_near:
         copy.start()
-
-    for t in range(12):
-        tile = gfull[:, t * BLK:(t + 1) * BLK].T
-        for n in range(8):
-            row = t * BLK + n * 16
-            gt[row // 192, (row % 192) // 48, row % 48:row % 48 + 16, :] = tile[n * 16:(n + 1) * 16]
-    gy_remote = []
-    for m in range(1, 8):
-        p = (pos + m) % 8
-        gy_remote.append(rcopy(gt.at[:, p // 2], gy.at[:, :, lanes(pos)], s_gy.at[m], r_gy.at[pos], ydev(p)))
-    gy_local = lcopy(gt.at[:, y], gy.at[:, :, lanes(pos)], r_gy.at[pos])
-
-    x_fwd = forward_shared(xt, rx, s_xf, r_xc)
-    for copy in gy_remote:
-        copy.start()
-    gy_local.start()
     wait_own(xt, rx, r_xa, r_xc)
 
     def naturals(slot):
@@ -234,6 +259,10 @@
         slot = i // 4
         qb = jnp.where(i < 4, i, shared_block(2 * (i % 2)) // 2)
 
+        @pl.when(i == 2)
+        def _():
+            forward_shared(xt, rx, s_xf, r_xc)
+
         @pl.when(i == 4)
         def _():
             for copy in at_remote:
@@ -269,8 +298,21 @@
 
     atc("start")
 
-    d_fwd = forward_shared(dat, rd, s_df, r_dc)
-    wait_shared(dat, rd, r_dc)
+    gsend.wait_recv()
+    other_cols = pl.ds(pl.multiple_of((1 - hd) * FEAT, BLK), FEAT)
+    for t in range(3):
+        rows = slice(t * QB, (t + 1) * QB)
+        part = (dpart[rows, :] + mm(w_ref[rows, other_cols], gfull[:, other_cols], 1, 1)).astype(BF)
+        for n in range(4):
+            dat[4 * t + n] = part[n * HD:(n + 1) * HD]
+    d_remote, d_local = scatter_plan(dat, rd, s_d, r_da, r_dc)
+    for copy in d_remote + d_local:
+        copy.start()
+    gy_far_fwd = gy_forward(hd, 0)
+    transposed_half(1 - hd)
+    gy_far = gy_plan(1 - hd, 1)
+    for copy in gy_far:
+        copy.start()
     acc[...] = jnp.zeros_like(acc)
 
     half_there = pl.ds(pl.multiple_of((1 - c) * 512, BLK), 512)
@@ -282,9 +324,23 @@
             b = shared_block(n)
             shared_send(dqkv.at[1, 0, :, lanes(b)], rout.at[3 * j + 2, 0], s_oq, r_oq.at[3 * j + 2], n, b, op)
 
+    ready = {3: (), 2: (5, 6, 7), 1: (3, 4), 0: (0, 1, 2)}
+
+    def own_send(b, op):
+        shared_send(dqkv.at[0, :, :, lanes(b)], rout.at[3 * j + c], s_o, r_o.at[3 * j + c], b, b, op)
+
+    def finish(n):
+        if not ready[n]:
+            return
+        span = slice(ready[n][0] * BLK, (ready[n][-1] + 1) * BLK)
+        dqkv[0, 1, :, span] = (acc[0, 0, :, span] * HD ** (-0.5)).astype(BF)
+        dqkv[0, 2, :, span] = acc[0, 1, :, span].astype(BF)
+        for b in ready[n]:
+            own_send(b, "start")
+
     def bwd_item(i, carry):
         slot = jnp.where(i < 2, 1, 0)
-        qb = jnp.where(i < 2, shared_block(2 * (i % 2)) // 2, i - 2)
+        qb = jnp.where(i < 2, shared_block(2 * (i % 2)) // 2, 5 - i)
 
         @pl.when(i == 2)
         def _():
@@ -297,24 +353,28 @@
             def _(n=n):
                 backward(n, slot)
 
+                @pl.when(slot == 0)
+                def _():
+                    finish(n)
+
         return carry
 
-    lax.fori_loop(0, 2, bwd_item, 0)
-    for h in range(12):
-        lcopy(att.at[0], att.at[h], r_at.at[h]).wait()
-    for t in range(6):
-        tile = att[2 * t:2 * t + 2].reshape(BLK, BLK).T
-        attn[t // 3, :, (t % 3) * BLK:(t % 3 + 1) * BLK] = tile
     ay_remote = []
-    for m in range(1, 8):
-        p = (pos + m) % 8
-        ay_remote.append(
-            rcopy(attn.at[p % 2], ay.at[pl.ds(pl.multiple_of(pos * BLK, BLK), BLK), :], s_ay.at[m], r_ay.at[pos], ydev(p))
-        )
-    ay_local = lcopy(attn.at[c], ay.at[pl.ds(pl.multiple_of(pos * BLK, BLK), BLK), :], r_ay.at[pos])
-    for copy in ay_remote:
-        copy.start()
-    ay_local.start()
+    for part, tiles in enumerate(((0,), (1, 2))):
+        for core in range(2):
+            for t in tiles:
+                t = 3 * core + t
+                for h in (2 * t, 2 * t + 1):
+                    lcopy(att.at[0], att.at[h], r_at.at[h]).wait()
+                tile = att[2 * t:2 * t + 2].reshape(BLK, BLK).T
+                attn[core, :, (t % 3) * BLK:(t % 3 + 1) * BLK] = tile
+        cols = pl.ds(tiles[0] * BLK, len(tiles) * BLK)
+        rows = pl.ds(pl.multiple_of(pos * BLK, BLK), BLK)
+        dst = (ay0, ay1)[part].at[rows, :]
+        for n, (core, dev) in enumerate(((0, ydev(0)), (1, ydev(1)), (1 - c, sib))):
+            ay_remote.append(rcopy(attn.at[core, :, cols], dst, s_ay.at[part, n], r_ay.at[part, pos], dev))
+            ay_remote[-1].start()
+        lcopy(attn.at[c, :, cols], dst, r_ay.at[part, pos]).start()
 
     def project(half):
         cols = pl.ds(pl.multiple_of(half * FEAT, BLK), FEAT)
@@ -325,19 +385,30 @@
     p_copy.start()
     pown[...] = project(hd)
 
+    forward_shared(dat, rd, s_df, r_dc)
+    wait_shared(dat, rd, r_dc)
+    lax.fori_loop(0, 2, bwd_item, 0)
+    gy_far_fwd += gy_forward(1 - hd, 1)
+    for which, half in ((0, hd), (1, 1 - hd)):
+        gy_wait(half, which, pos)
+        for g in range(2):
+            gy_wait(half, which, g * 2 + 1 - c)
+    z_remote = []
+    for part, (ayp, dp, zp, rzp) in enumerate(((ay0, df0, zs0, rz0), (ay1, df1, zs1, rz1))):
+        for p in range(4):
+            rows = pl.ds(p * BLK, BLK)
+            lcopy(ayp.at[rows, :], ayp.at[rows, :], r_ay.at[part, p]).wait()
+        for t in range(2):
+            sums = mm(gy[4 * t:4 * t + 4].reshape(384, 512), ayp[...], 1, 0)
+            sums = sums.reshape(4, 96, sums.shape[1])
+            dp[4 * t:4 * t + 4] = sums
+            zp[4 * t:4 * t + 4] = sums.astype(BF)
+        for m in range(1, 8):
+            zz = (z + m) % 8
+            z_remote.append(rcopy(zp.at[zz], rzp.at[z], s_z.at[part, m], r_z.at[part, z], zdev(zz)))
+            z_remote[-1].start()
+
     lax.fori_loop(2, 6, bwd_item, 0)
-    for i in range(2):
-        scale = HD ** (-0.5) if i == 0 else 1.0
-        dqkv[0, 1 + i] = (acc[0, i] * scale).astype(BF)
-    o_remote = []
-    for m in range(1, 8):
-        b = (s + m) % 8
-        o_remote.append(rcopy(dqkv.at[0, :, :, lanes(b)], rout.at[3 * j + c], s_o.at[m], r_o.at[3 * j + c], clip8 + b))
-    o_local = lcopy(dqkv.at[0, :, :, lanes(s)], rout.at[3 * j + c], r_o.at[3 * j + c])
-    for copy in o_remote:
-        copy.start()
-    o_local.start()
-
     xc_copy.wait_recv()
     for i in range(2):
         scale = HD ** (-0.5) if i == 0 else 1.0
@@ -349,20 +420,6 @@
             shared_send(src, rout.at[3 * j + 2, 1:3], s_okv, r_o.at[3 * j + 2], n, 4 * c + n, op)
 
     okv("start")
-
-    for p in range(8):
-        lcopy(gt.at[:, 0], gy.at[:, :, lanes(p)], r_gy.at[p]).wait()
-        lcopy(attn.at[0], ay.at[p * BLK:(p + 1) * BLK, :], r_ay.at[p]).wait()
-    for t in range(2):
-        part = mm(gy[4 * t:4 * t + 4].reshape(192, SLOTS), ay[...], 1, 0)
-        dfull[4 * t:4 * t + 4] = part.reshape(4, 48, 384)
-    zs[...] = dfull[...].astype(BF)
-    z_remote = []
-    for m in range(1, 8):
-        zz = (z + m) % 8
-        z_remote.append(rcopy(zs.at[zz], rz.at[z], s_z.at[m], r_z.at[z], zdev(zz)))
-    for copy in z_remote:
-        copy.start()
 
     p_copy.wait_recv()
     proj_ref[...] = (pown[...] + precv[...].astype(F32)).astype(BF)
@@ -377,52 +434,62 @@
             tile = rout[2 * t:2 * t + 2, i].reshape(BLK, BLK)
             ref[:, t * BLK:(t + 1) * BLK] = tile.T
 
-    summed = dfull[z]
-    for m in range(1, 8):
-        zz = (z + m) % 8
-        lcopy(zs.at[0], rz.at[zz], r_z.at[zz]).wait()
-        summed = summed + rz[zz].astype(F32)
-    fin[...] = summed.reshape(2, 24, 384)
-    mine = xl * 2 + c
     f_remote = []
-    for m in range(1, 4):
-        t = (mine + m) % 4
-        f_remote.append(
-            rcopy(fin.at[t // 2], rf.at[mine], s_f.at[m], r_f.at[mine], me - mine + t)
-        )
-    for copy in f_remote:
-        copy.start()
-    rf[mine] = fin[xl]
-    for m in range(1, 4):
-        t = (mine + m) % 4
-        lcopy(fin.at[0], rf.at[t], r_f.at[t]).wait()
-    for cc in range(2):
-        both = rf[cc] + rf[2 + cc]
-        dw_ref[:, cc * 384:(cc + 1) * 384] = jnp.where(c == 0, both[:12], both[12:]).astype(BF)
+    for part, (dp, rzp, fp, rfp) in enumerate(((df0, rz0, fin0, rf0), (df1, rz1, fin1, rf1))):
+        summed = dp[z]
+        for m in range(1, 8):
+            zz = (z + m) % 8
+            lcopy(rzp.at[zz], rzp.at[zz], r_z.at[part, zz]).wait()
+            summed = summed + rzp[zz].astype(F32)
+        for t in range(8):
+            fp[t, :12, :] = summed[12 * t:12 * t + 12]
+        for m in range(1, 8):
+            t = (s + m) % 8
+            f_remote.append(rcopy(fp.at[t], rfp.at[s], s_f.at[part, m], r_f.at[part, s], clip8 + t))
+            f_remote[-1].start()
+        rfp[s] = fp[s]
+    for part, (rfp, lo, hi) in enumerate(((rf0, 0, BLK), (rf1, BLK, 3 * BLK))):
+        for m in range(1, 8):
+            t = (s + m) % 8
+            lcopy(rfp.at[t], rfp.at[t], r_f.at[part, t]).wait()
+        for core in range(2):
+            every = rfp[core] + rfp[2 + core] + rfp[4 + core] + rfp[6 + core]
+            dw_ref[:, core * 384 + lo:core * 384 + hi] = every[:12].astype(BF)
 
     gsend.wait_send()
-    for copy in x_remote + d_remote + x_fwd + d_fwd + gy_remote + at_remote + ay_remote + o_remote + z_remote + f_remote:
+    for copy in d_remote + shared_plan(rx, s_xf, r_xc) + shared_plan(rd, s_df, r_dc) + gy_near[:2] + gy_far[:2] + gy_far_fwd + at_remote + ay_remote + z_remote + f_remote:
         copy.wait_send()
     xc_copy.wait_send()
     p_copy.wait_send()
     atc("wait")
     oq("wait")
+    for b in range(8):
+        own_send(b, "wait")
     okv("wait")
+
+
+def place(*refs):
+    for i in range(5):
+        refs[5 + i][...] = refs[i][...]
 
 
 def local(queries, keys, values, w_out, grad_proj, frame_levels):
     vmem = pl.BlockSpec(memory_space=pltpu.VMEM)
     smem = pl.BlockSpec(memory_space=pltpu.SMEM)
+    hbm = pl.BlockSpec(memory_space=pl.ANY)
     rows = jax.ShapeDtypeStruct((BLK, FEAT), BF)
-    dma = lambda n: pltpu.SemaphoreType.DMA((n,))
-    scratch = [
+    dma = lambda n: pltpu.SemaphoreType.DMA(n if isinstance(n, tuple) else (n,))
+    scratch = [pltpu.VMEM((BLK, FEAT), BF)] * 3 + [
+        pltpu.VMEM((FEAT, WIDTH), BF),
+        pltpu.VMEM((BLK, FEAT), BF),
+        dma(5),
         pltpu.VMEM((12, 3, HD, BLK), BF),
         pltpu.VMEM((2, 3, HD, SLOTS), BF),
         pltpu.VMEM((12, HD, BLK), BF),
         pltpu.VMEM((2, HD, SLOTS), BF),
         pltpu.VMEM((BLK, WIDTH), BF),
         pltpu.VMEM((8, 4, 48, BLK), BF),
-        pltpu.VMEM((8, 48, SLOTS), BF),
+        pltpu.VMEM((8, 2, 48, 512), BF),
         pltpu.VMEM((2, 2, SLOTS, HD), BF),
         pltpu.VMEM((1, SLOTS), jnp.int32),
         pltpu.VMEM((2, 4, SLOTS, QB), F32),
@@ -439,30 +506,44 @@
         pltpu.VMEM((2, 3, HD, SLOTS), BF),
         pltpu.VMEM((2, HD, 512), BF),
         pltpu.VMEM((12, 3, HD, BLK), BF),
-        pltpu.VMEM((SLOTS, 384), BF),
-        pltpu.VMEM((8, 48, 384), F32),
-        pltpu.VMEM((8, 48, 384), BF),
-        pltpu.VMEM((8, 48, 384), BF),
-        pltpu.VMEM((2, 24, 384), F32),
-        pltpu.VMEM((4, 24, 384), F32),
+        pltpu.VMEM((FEAT, BLK), F32),
+    ] + [
+        pltpu.VMEM(lead + (n * BLK,), kind)
+        for lead, kind in (
+            ((512,), BF),
+            ((8, 96), F32),
+            ((8, 96), BF),
+            ((8, 96), BF),
+            ((8, 16), F32),
+            ((8, 16), F32),
+        )
+        for n in (1, 2)
     ] + [
         dma(n)
         for n in (
-            11, 3, 8, 8, 11, 3, 8, 8, 2, 1, 8, 8,
-            8, 4, 12, 8, 8, 1, 1, 1, 1, 8, 4, 4, 12, 12,
-            8, 8, 4, 4,
+            11, 3, 8, 8, 11, 3, 8, 8, 1, 1, (2, 3), (2, 4),
+            8, 4, 12, (2, 3), (2, 4), 1, 1, 1, 1, 8, 4, 4, 12, 12,
+            (2, 8), (2, 8), (2, 8), (2, 8),
         )
     ]
     proj, dq, dk, dv, dw = pl.pallas_call(
         kernel,
         out_shape=(rows, rows, rows, rows, jax.ShapeDtypeStruct((12, FEAT), BF)),
-        in_specs=[vmem] * 5 + [smem],
+        in_specs=[hbm] * 5 + [smem],
         out_specs=[vmem] * 5,
         scratch_shapes=scratch,
         compiler_params=pltpu.CompilerParams(
             collective_id=0, has_side_effects=True, vmem_limit_bytes=56 * 1024 * 1024
         ),
     )(queries, keys, values, w_out, grad_proj, frame_levels)
+    strict = pl.BlockSpec(memory_space=pltpu.HBM)
+    proj, dq, dk, dv, dw = pl.pallas_call(
+        place,
+        out_shape=(rows,) * 4 + (jax.ShapeDtypeStruct((12, FEAT), BF),),
+        in_specs=[vmem] * 5,
+        out_specs=[vmem] * 5,
+        scratch_shapes=[],
+    )(proj, dq, dk, dv, dw)
     return proj, dq, dk, dv, dw.T
 
 

time: 72 us -> 56.5 us (0.78)
  local copies, waits for them, and re-layouts: 7.81 us -> 0 us
  Pallas kernels: 63.3 us -> 55.7 us
    pallas_call x1, Pallas kernels: 63.3 us -> 53.6 us  [local(): pl.pallas_call(kernel, out_shape=(rows, rows, rows, rows, jax.ShapeDtypeS...]
    unnamed x5 -> x0, local copies, waits for them, and re-layouts: 7.81 us -> none
    pallas_call x0 -> x1, Pallas kernels: none -> 2.11 us  [local(): pl.pallas_call(place, out_shape=(rows,) * 4 + (jax.ShapeDtypeStruct((12,...]
where the time goes in v2:
time: 56.5 us; the launch traced here: 56.3 us
  Pallas kernels  55.7 us (99%)
  between operations  0.64 us (1%)
    pallas_call x1, Pallas kernels, local(): pl.pallas_call(kernel, out_shape=(rows, rows, rows, rows, jax.ShapeDtypeS...  53.6 us
    pallas_call x1, Pallas kernels, local(): pl.pallas_call(place, out_shape=(rows,) * 4 + (jax.ShapeDtypeStruct((12,...  2.11 us

profile of v2, /device:TPU:1, one launch (start us, length us, event | category | flops | bytes accessed | tf_op | source)
XLA Modules:
  0.0 56.3 jit_solution(16243709013850886205)
XLA Ops:
  0.6 53.6 %shard_map.101 = (bf16[128,768]{1,0:T(8,128)(2,1)}, bf16[128,768]{1,0:T(8,128)(2,1)}, bf16[128,768]{1,0:T(8,128)(2,1)}, bf16[128,768]{1,0:T(8,128)(2,1)}, bf16[12,768]{1,0:T(8,128)(2,1)}) custom-call(bf16[128,768]{1,0:T(8,128)(2,1)} %q_hbm.1, bf16[128,768]{1,0:T(8,128)(2,1)} %k_hbm.1, bf16[128,768]{1,0:T(8,128)(2,1)} %v_hbm.1, bf16[768,1536]{1,0:T(8,128)(2,1)} %w_hbm.1, ...), custom_call_target="tpu_custom_call" | custom-call | tf_op jit(solution)/shard_map/pallas_call | solution.py:529
  54.2 2.1 %shard_map.102 = (bf16[128,768]{1,0:T(8,128)(2,1)}, bf16[128,768]{1,0:T(8,128)(2,1)}, bf16[128,768]{1,0:T(8,128)(2,1)}, bf16[128,768]{1,0:T(8,128)(2,1)}, bf16[12,768]{1,0:T(8,128)(2,1)}) custom-call(bf16[128,768]{1,0:T(8,128)(2,1)} %get-tuple-element.15.refs_0_, bf16[128,768]{1,0:T(8,128)(2,1)} %get-tuple-element.16.refs_1_, ...), custom_call_target="tpu_custom_call" | custom-call | tf_op jit(solution)/shard_map/pallas_call | solution.py:540

commit v3 on v2

v3 whole, which is shorter than its diff:
```python
import functools
import math

import jax
import jax.numpy as jnp
from jax import lax
from jax.experimental import pallas as pl
from jax.experimental.pallas import tpu as pltpu
from jax.sharding import PartitionSpec as P

MESH = pl.DeviceIdType.MESH
BF = jnp.bfloat16
F32 = jnp.float32
HD = 64
BLK = 128
QB = 256
SLOTS = 1024
FEAT = 768
WIDTH = 1536
FRAMES_CLIP = 16
EXP_SCALE = HD ** (-0.5) * math.log2(math.e)


def mm(left, right, dl, dr):
    return lax.dot_general(left, right, (((dl,), (dr,)), ((), ())), preferred_element_type=F32)


def lanes(block):
    return pl.ds(pl.multiple_of(block * BLK, BLK), BLK)


def kernel(
    q_hbm, k_hbm, v_hbm, w_hbm, g_hbm, lev_ref,
    proj_hbm, dq_hbm, dk_hbm, dv_hbm, dw_ref,
    proj_ref, dq_ref, dk_ref, dv_ref, s_out, q_ref, k_ref, v_ref, w_ref, g_ref, s_in, xt, rx, dat, rd, gfull, gt, gy, nat, lim_ref, inv_ref, prob, low, dsb,
    ot, att, attn, pown, psend, precv, acc, xc, dqkv, dkvc, rout,
    dpart, ayt, df, zs, rz, fin, rf,
    s_x, s_xf, r_xa, r_xc, s_d, s_df, r_da, r_dc, s_g, r_g, s_gy, r_gy,
    s_at, r_at, s_ay, r_ay, s_p, r_p, s_xc, r_xc2, s_o, s_oq, s_okv, r_o, r_oq,
    s_z, r_z, s_f, r_f,
):
    me = lax.axis_index("frame")
    hd = lax.axis_index("head")
    c = me % 2
    xl = (me // 2) % 2
    y = (me // 4) % 4
    z = me // 16
    s = me % 8
    clip8 = me - s
    j = s // 2
    sib = me + 1 - 2 * c
    far_y = 3 - y
    group = y // 2
    pos = group * 2 + c
    others = (3 - j, j + 1 - 2 * (j % 2), (j + 2) % 4)

    def rcopy(src, dst, ss, rs, dev, head=hd):
        return pltpu.make_async_remote_copy(
            src_ref=src, dst_ref=dst, send_sem=ss, recv_sem=rs,
            device_id=(dev, head), device_id_type=MESH,
        )

    def lcopy(src, dst, sem):
        return pltpu.make_async_copy(src, dst, sem)

    def ydev(core):
        return z * 16 + far_y * 4 + xl * 2 + core

    def zdev(zz):
        return zz * 16 + me % 16

    loads = [
        lcopy(src, dst, s_in.at[i])
        for i, (src, dst) in enumerate(
            ((q_hbm, q_ref), (k_hbm, k_ref), (v_hbm, v_ref), (g_hbm, g_ref), (w_hbm, w_ref))
        )
    ]
    for copy in loads:
        copy.start()

    bar = pltpu.get_barrier_semaphore()
    for d in range(1, 8):
        pl.semaphore_signal(bar, inc=1, device_id=(clip8 + (s + d) % 8, hd), device_id_type=MESH)
    pl.semaphore_signal(bar, inc=1, device_id=(me, 1 - hd), device_id_type=MESH)
    for core in range(2):
        pl.semaphore_signal(bar, inc=1, device_id=(ydev(core), hd), device_id_type=MESH)
    for d in (1, 2, 6, 7):
        pl.semaphore_signal(bar, inc=1, device_id=(zdev((z + d) % 8), hd), device_id_type=MESH)

    for i, ref in enumerate((q_ref, k_ref, v_ref)):
        loads[i].wait()
        for t in range(6):
            tile = ref[:, t * BLK:(t + 1) * BLK].T
            xt[2 * t, i] = tile[:HD]
            xt[2 * t + 1, i] = tile[HD:]
    pl.semaphore_wait(bar, 14)

    def scatter_plan(src, dst, ss, ra, rc):
        remote = []
        shared = []
        for n, jj in enumerate(others):
            base = clip8 + jj * 2
            remote.append(rcopy(src.at[3 * jj], dst.at[0, ..., lanes(s)], ss.at[3 * n], ra.at[s], base))
            remote.append(rcopy(src.at[3 * jj + 1], dst.at[0, ..., lanes(s)], ss.at[3 * n + 1], ra.at[s], base + 1))
            shared.append(rcopy(src.at[3 * jj + 2], dst.at[1, ..., lanes(s)], ss.at[3 * n + 2], rc.at[s], base + c))
        remote.append(rcopy(src.at[3 * j + 1 - c], dst.at[0, ..., lanes(s)], ss.at[9], ra.at[s], sib))
        shared.append(rcopy(src.at[3 * j + 2], dst.at[1, ..., lanes(s)], ss.at[10], rc.at[s], sib))
        local = [
            lcopy(src.at[3 * j + c], dst.at[0, ..., lanes(s)], ra.at[s]),
            lcopy(src.at[3 * j + 2], dst.at[1, ..., lanes(s)], rc.at[s]),
        ]
        return remote + shared, local

    def wait_own(src, dst, ra, rc):
        for b in range(8):
            lcopy(src.at[0], dst.at[0, ..., lanes(b)], ra.at[b]).wait()

    def shared_plan(dst, fs, rc):
        return [
            rcopy(dst.at[1, ..., lanes(jj * 2 + c)], dst.at[1, ..., lanes(jj * 2 + c)], fs.at[n], rc.at[jj * 2 + c], sib)
            for n, jj in enumerate(others)
        ]

    def forward_shared(src, dst, fs, rc):
        for copy, jj in zip(shared_plan(dst, fs, rc), others):
            lcopy(src.at[0], dst.at[1, ..., lanes(jj * 2 + c)], rc.at[jj * 2 + c]).wait()
            copy.start()
        lcopy(src.at[0], dst.at[1, ..., lanes(s)], rc.at[s]).wait()

    def wait_shared(src, dst, rc):
        for jj in range(4):
            b = jj * 2 + 1 - c
            lcopy(src.at[0], dst.at[1, ..., lanes(b)], rc.at[b]).wait()

    x_remote, x_local = scatter_plan(xt, rx, s_x, r_xa, r_xc)
    for copy in x_remote + x_local:
        copy.start()

    slot_iota = lax.broadcasted_iota(jnp.int32, (1, SLOTS), 1)
    seen = jnp.zeros((1, SLOTS), jnp.int32)
    start = jnp.int32(0)
    for f in range(FRAMES_CLIP):
        level = lev_ref[(me // 8) * FRAMES_CLIP + f]
        end = start + jnp.where(level == 0, BLK, jnp.where(level == 1, BLK // 4, BLK // 16))
        seen = jnp.where((slot_iota >= start) & (slot_iota < end), end, seen)
        start = end
    lim_ref[...] = seen

    def transposed_half(half):
        for t in range(6):
            cols = pl.ds(pl.multiple_of(half * FEAT + t * BLK, BLK), BLK)
            tile = gfull[:, cols].T
            for n in range(8):
                row = t * BLK + n * 16
                gt[4 * half + row // 192, (row % 192) // 48, row % 48:row % 48 + 16, :] = tile[n * 16:(n + 1) * 16]

    def gt_part(half, which_group):
        return gt.at[pl.ds(4 * half, 4), pl.ds(2 * which_group, 2)]

    def gy_part(half, p):
        return gy.at[pl.ds(4 * half, 4), :, :, lanes(p)]

    def gy_plan(half, which):
        return [
            rcopy(gt_part(half, 1 - group), gy_part(half, pos), s_gy.at[which, 0], r_gy.at[which, pos], ydev(c)),
            rcopy(gt_part(half, group), gy_part(half, pos), s_gy.at[which, 1], r_gy.at[which, pos], sib),
            lcopy(gt_part(half, group), gy_part(half, pos), r_gy.at[which, pos]),
        ]

    def gy_wait(half, which, p):
        lcopy(gt_part(half, group), gy_part(half, p), r_gy.at[which, p]).wait()

    def gy_forward(half, which):
        p = (1 - group) * 2 + c
        gy_wait(half, which, p)
        copy = rcopy(gy_part(half, p), gy_part(half, p), s_gy.at[which, 2], r_gy.at[which, p], sib)
        copy.start()
        return [copy]

    loads[3].wait()
    own_cols = pl.ds(pl.multiple_of(hd * FEAT, BLK), FEAT)
    gfull[:, own_cols] = g_ref[...]
    transposed_half(hd)
    loads[4].wait()
    for t in range(3):
        dpart[t * QB:(t + 1) * QB, :] = mm(w_ref[t * QB:(t + 1) * QB, own_cols], g_ref[...], 1, 1)
    for copy in x_remote:
        copy.wait_send()
    gsend = rcopy(g_ref, gfull.at[:, own_cols], s_g.at[0], r_g.at[0], me, 1 - hd)
    gsend.start()
    gy_near = gy_plan(hd, 0)
    for copy in gy_near:
        copy.start()
    wait_own(xt, rx, r_xa, r_xc)

    def naturals(slot):
        for i in range(2):
            nat[slot, i] = rx[slot, 1 + i].T

    naturals(0)

    def forward(ns, slot):
        q0s = [n * QB for n in ns]
        nks = [min(2 * n + 3, 8) for n in ns]
        qts = [rx[slot, 0, :, q0:q0 + QB] for q0 in q0s]
        lims = [lim_ref[:, q0:q0 + QB] for q0 in q0s]
        peaks = [jnp.full((8, QB), -1e30, F32) for _ in ns]
        work = [(kc, p) for kc in range(8) for p in range(2) if kc < nks[p]]
        for kc, p in work:
            rows = slice(kc * BLK, (kc + 1) * BLK)
            sc = mm(nat[slot, 0, rows, :], qts[p], 1, 0)
            if kc * BLK >= q0s[p]:
                key = lax.broadcasted_iota(jnp.int32, (BLK, QB), 0) + kc * BLK
                sc = jnp.where(key < lims[p], sc, -1e30)
            prob[slot, ns[p], rows, :] = sc
            peaks[p] = jnp.maximum(peaks[p], jnp.max(sc.reshape(BLK // 8, 8, QB), axis=0))
        peaks = [jnp.max(peak, axis=0, keepdims=True) for peak in peaks]
        totals = [jnp.zeros((8, QB), F32) for _ in ns]
        for kc, p in work:
            rows = slice(kc * BLK, (kc + 1) * BLK)
            ex = jnp.exp2((prob[slot, ns[p], rows, :] - peaks[p]) * EXP_SCALE)
            prob[slot, ns[p], rows, :] = ex
            totals[p] = totals[p] + jnp.sum(ex.reshape(BLK // 8, 8, QB), axis=0)
        totals = [jnp.sum(total, axis=0, keepdims=True) for total in totals]
        invs = [jnp.where(lim > 0, 1.0 / total, 0.0) for lim, total in zip(lims, totals)]
        for p in range(2):
            inv_ref[slot, :, q0s[p]:q0s[p] + QB] = invs[p]
        for kc, p in work:
            rows = slice(kc * BLK, (kc + 1) * BLK)
            low[slot, ns[p], rows, :] = (prob[slot, ns[p], rows, :] * invs[p]).astype(BF)
        for p in range(2):
            kl = nks[p] * BLK
            ot[slot, :, q0s[p]:q0s[p] + QB] = mm(rx[slot, 2, :, :kl], low[slot, ns[p], :kl, :], 1, 0).astype(BF)

    def backward(ns, slot):
        q0s = [n * QB for n in ns]
        nks = [min(2 * n + 3, 8) for n in ns]
        qts = [rx[slot, 0, :, q0:q0 + QB] for q0 in q0s]
        das = [rd[slot, :, q0:q0 + QB] for q0 in q0s]
        invs = [inv_ref[slot, :, q0:q0 + QB] for q0 in q0s]
        deltas = [
            jnp.sum(da.astype(F32) * ot[slot, :, q0:q0 + QB].astype(F32), axis=0, keepdims=True)
            for da, q0 in zip(das, q0s)
        ]
        for kc in range(8):
            rows = slice(kc * BLK, (kc + 1) * BLK)
            for p in range(2):
                if kc < nks[p]:
                    dp = mm(nat[slot, 1, rows, :], das[p], 1, 0)
                    dsb[p, rows, :] = (prob[slot, ns[p], rows, :] * invs[p] * (dp - deltas[p])).astype(BF)
        for p in range(2):
            kl = nks[p] * BLK
            dq = mm(rx[slot, 1, :, :kl], dsb[p, :kl, :], 1, 0) * HD ** (-0.5)
            dqkv[slot, 0, :, q0s[p]:q0s[p] + QB] = dq.astype(BF)
        for p in range(2):
            kl = nks[p] * BLK
            acc[slot, 0, :, :kl] += mm(qts[p], dsb[p, :kl, :], 1, 1)
            acc[slot, 1, :, :kl] += mm(das[p], low[slot, ns[p], :kl, :], 1, 1)

    def shared_send(src, dst, ss, rs, n, block, op):
        @pl.when(block == s)
        def _():
            if op == "start":
                lcopy(src, dst, rs).start()

        @pl.when(block != s)
        def _():
            copy = rcopy(src, dst, ss.at[n], rs, clip8 + block)
            copy.start() if op == "start" else copy.wait_send()

    def at_send(slot, n, op):
        head = 3 * j + c + slot * (2 - c)
        for b in (2 * n, 2 * n + 1):
            shared_send(ot.at[slot, :, lanes(b)], att.at[head], s_at.at[slot], r_at.at[head], b, b, op)

    def shared_block(n):
        return (1 - c) * (n + 4 * (n // 2)) + c * (n + 2)

    pairs = ((0, 3), (1, 2))

    def fwd_item(i, carry):
        slot = i // 2
        pair = jnp.where(i < 2, i, c)

        @pl.when(i == 1)
        def _():
            forward_shared(xt, rx, s_xf, r_xc)

        @pl.when(i == 2)
        def _():
            wait_shared(xt, rx, r_xc)
            naturals(1)

        for n in range(2):
            @pl.when(pair == n)
            def _(n=n):
                forward(pairs[n], slot)
                for qb in pairs[n]:
                    at_send(slot, qb, "start")

        return carry

    lax.fori_loop(0, 3, fwd_item, 0)

    acc[...] = jnp.zeros_like(acc)
    half_there = pl.ds(pl.multiple_of((1 - c) * 512, BLK), 512)
    half_here = pl.ds(pl.multiple_of(c * 512, BLK), 512)
    xc_copy = rcopy(acc.at[1, :, :, half_there], xc, s_xc.at[0], r_xc2.at[0], sib)

    def oq(op):
        for n in range(4):
            b = shared_block(n)
            shared_send(dqkv.at[1, 0, :, lanes(b)], rout.at[3 * j + 2, 0], s_oq, r_oq.at[3 * j + 2], n, b, op)

    def okv(op):
        for n in range(4):
            src = dkvc.at[:, :, n * BLK:(n + 1) * BLK]
            shared_send(src, rout.at[3 * j + 2, 1:3], s_okv, r_o.at[3 * j + 2], n, 4 * c + n, op)

    def own_send(b, op):
        shared_send(dqkv.at[0, :, :, lanes(b)], rout.at[3 * j + c], s_o, r_o.at[3 * j + c], b, b, op)

    def finish():
        dqkv[0, 1] = (acc[0, 0] * HD ** (-0.5)).astype(BF)
        dqkv[0, 2] = acc[0, 1].astype(BF)
        for b in range(8):
            own_send(b, "start")

    def bwd_item(i, carry):
        slot = jnp.where(i == 0, 1, 0)
        pair = jnp.where(i == 0, c, i - 1)

        @pl.when(i == 1)
        def _():
            xc_copy.start()
            oq("start")
            wait_own(dat, rd, r_da, r_dc)

        @pl.when(i == 2)
        def _():
            xc_copy.wait_recv()
            for part in range(2):
                scale = HD ** (-0.5) if part == 0 else 1.0
                dkvc[part] = ((acc[1, part, :, half_here] + xc[part]) * scale).astype(BF)
            okv("start")

        for n in range(2):
            @pl.when(pair == n)
            def _(n=n):
                backward(pairs[n], slot)

        return carry

    ay_remote = []

    def attended_part(part):
        for core in range(2):
            for h in range(2):
                lcopy(att.at[0], att.at[6 * core + 2 * part + h], r_at.at[6 * core + 2 * part + h]).wait()
        dst = ayt.at[part, :, :, lanes(pos)]
        for n, (core, dev) in enumerate(((0, ydev(0)), (1, ydev(1)), (1 - c, sib))):
            src = att.at[pl.ds(6 * core + 2 * part, 2)]
            ay_remote.append(rcopy(src, dst, s_ay.at[part, n], r_ay.at[part, pos], dev))
            ay_remote[-1].start()
        lcopy(att.at[pl.ds(6 * c + 2 * part, 2)], dst, r_ay.at[part, pos]).start()

    def attended_rows():
        for t in range(6):
            tile = att[2 * t:2 * t + 2].reshape(BLK, BLK).T
            attn[t // 3, :, (t % 3) * BLK:(t % 3 + 1) * BLK] = tile

    first_hops = ((4, 2, 0), (3, 1, 1), (5, 7, 2), (1, 1, 3), (7, 7, 4))
    second_hops = ((2, 2, 5, (0, 1)), (6, 6, 6, (2,)))

    def z_copy(owner, to, slot):
        return rcopy(zs.at[(z + owner) % 8], rz.at[slot], s_z.at[slot], r_z.at[slot], zdev((z + to) % 8))

    def z_arrived(slot):
        lcopy(rz.at[slot], rz.at[slot], r_z.at[slot]).wait()

    def z_first(half):
        for owner, to, slot in first_hops:
            @pl.when(((z + owner) % 8) // 4 == half)
            def _():
                z_copy(owner, to, slot).start()

    def z_second():
        for owner, to, slot, joined in second_hops:
            piece = df[(z + owner) % 8]
            for n in joined:
                z_arrived(n)
                piece = piece + rz[n].astype(F32)
            zs[(z + owner) % 8] = piece.astype(BF)
            z_copy(owner, to, slot).start()

    def gy_arrived(half, which):
        gy_wait(half, which, pos)
        for g in range(2):
            gy_wait(half, which, g * 2 + 1 - c)

    def ay_arrived(part):
        for p in range(4):
            dst = ayt.at[part, :, :, lanes(p)]
            lcopy(dst, dst, r_ay.at[part, p]).wait()

    def weight_part(part, half):
        mine = pl.ds(4 * half, 4)
        heads = ayt[part].reshape(BLK, 512)
        sums = mm(gy[mine].reshape(384, 512), heads, 1, 1).reshape(4, 96, BLK)
        df[mine, part] = sums
        zs[mine, part] = sums.astype(BF)

    def project(half):
        cols = pl.ds(pl.multiple_of(half * FEAT, BLK), FEAT)
        return mm(attn[0], w_ref[:384, cols], 1, 0) + mm(attn[1], w_ref[384:, cols], 1, 0)

    attended_part(0)
    gsend.wait_recv()
    other_cols = pl.ds(pl.multiple_of((1 - hd) * FEAT, BLK), FEAT)
    for t in range(3):
        rows = slice(t * QB, (t + 1) * QB)
        part = (dpart[rows, :] + mm(w_ref[rows, other_cols], gfull[:, other_cols], 1, 1)).astype(BF)
        for n in range(4):
            dat[4 * t + n] = part[n * HD:(n + 1) * HD]
    d_remote, d_local = scatter_plan(dat, rd, s_d, r_da, r_dc)
    for copy in d_remote + d_local:
        copy.start()
    attended_part(1)
    attended_part(2)
    transposed_half(1 - hd)
    gy_far = gy_plan(1 - hd, 1)
    for copy in gy_far:
        copy.start()
    gy_far_fwd = gy_forward(hd, 0)
    forward_shared(dat, rd, s_df, r_dc)
    gy_arrived(hd, 0)
    for part in range(3):
        ay_arrived(part)
        weight_part(part, hd)
    z_first(hd)
    attended_rows()
    psend[...] = project(1 - hd).astype(BF)
    p_copy = rcopy(psend, precv, s_p.at[0], r_p.at[0], me, 1 - hd)
    p_copy.start()
    gy_far_fwd += gy_forward(1 - hd, 1)
    wait_shared(dat, rd, r_dc)
    lax.fori_loop(0, 1, bwd_item, 0)
    gy_arrived(1 - hd, 1)
    for part in range(3):
        weight_part(part, 1 - hd)
    z_first(1 - hd)
    lax.fori_loop(1, 3, bwd_item, 0)
    finish()
    z_second()
    pown[...] = project(hd)
    p_copy.wait_recv()
    proj_ref[...] = (pown[...] + precv[...].astype(F32)).astype(BF)
    stores = [lcopy(proj_ref, proj_hbm, s_out.at[3])]
    stores[0].start()

    for jj in range(4):
        for cc in range(2):
            lcopy(rout.at[0], rout.at[3 * jj + cc], r_o.at[3 * jj + cc]).wait()
        lcopy(rout.at[0, 0], rout.at[3 * jj + 2, 0], r_oq.at[3 * jj + 2]).wait()
        lcopy(rout.at[0, 1:3], rout.at[3 * jj + 2, 1:3], r_o.at[3 * jj + 2]).wait()
    for i, (ref, dst) in enumerate(((dq_ref, dq_hbm), (dk_ref, dk_hbm), (dv_ref, dv_hbm))):
        for t in range(6):
            tile = rout[2 * t:2 * t + 2, i].reshape(BLK, BLK)
            ref[:, t * BLK:(t + 1) * BLK] = tile.T
        stores.append(lcopy(ref, dst, s_out.at[i]))
        stores[-1].start()
    f_remote = []
    summed = df[z]
    for slot in range(3, 7):
        z_arrived(slot)
        summed = summed + rz[slot].astype(F32)
    for t in range(8):
        fin[t, :, :12, :] = summed[:, 12 * t:12 * t + 12]
    for m in range(1, 8):
        t = (s + m) % 8
        f_remote.append(rcopy(fin.at[t], rf.at[s], s_f.at[m], r_f.at[s], clip8 + t))
        f_remote[-1].start()
    rf[s] = fin[s]
    for m in range(1, 8):
        t = (s + m) % 8
        lcopy(rf.at[t], rf.at[t], r_f.at[t]).wait()
    for core in range(2):
        every = rf[core] + rf[2 + core] + rf[4 + core] + rf[6 + core]
        for part in range(3):
            lo = core * 384 + part * BLK
            dw_ref[:, lo:lo + BLK] = every[part, :12].astype(BF)
    for copy in stores:
        copy.wait()

    gsend.wait_send()
    for copy in d_remote + shared_plan(rx, s_xf, r_xc) + shared_plan(rd, s_df, r_dc) + gy_near[:2] + gy_far[:2] + gy_far_fwd + ay_remote + f_remote:
        copy.wait_send()
    xc_copy.wait_send()
    p_copy.wait_send()
    for n in range(4):
        at_send(0, n, "wait")

        @pl.when((c == 0) == (n in (0, 3)))
        def _(n=n):
            at_send(1, n, "wait")

    oq("wait")
    for b in range(8):
        own_send(b, "wait")
    okv("wait")
    for owner, to, slot in first_hops:
        z_copy(owner, to, slot).wait_send()
    for owner, to, slot, _ in second_hops:
        z_copy(owner, to, slot).wait_send()


def place(*refs):
    for i in range(5):
        refs[5 + i][...] = refs[i][...]


def local(queries, keys, values, w_out, grad_proj, frame_levels):
    vmem = pl.BlockSpec(memory_space=pltpu.VMEM)
    smem = pl.BlockSpec(memory_space=pltpu.SMEM)
    hbm = pl.BlockSpec(memory_space=pl.ANY)
    rows = jax.ShapeDtypeStruct((BLK, FEAT), BF)
    dma = lambda n: pltpu.SemaphoreType.DMA(n if isinstance(n, tuple) else (n,))
    scratch = [pltpu.VMEM((BLK, FEAT), BF)] * 4 + [dma(4)] + [pltpu.VMEM((BLK, FEAT), BF)] * 3 + [
        pltpu.VMEM((FEAT, WIDTH), BF),
        pltpu.VMEM((BLK, FEAT), BF),
        dma(5),
        pltpu.VMEM((12, 3, HD, BLK), BF),
        pltpu.VMEM((2, 3, HD, SLOTS), BF),
        pltpu.VMEM((12, HD, BLK), BF),
        pltpu.VMEM((2, HD, SLOTS), BF),
        pltpu.VMEM((BLK, WIDTH), BF),
        pltpu.VMEM((8, 4, 48, BLK), BF),
        pltpu.VMEM((8, 2, 48, 512), BF),
        pltpu.VMEM((2, 2, SLOTS, HD), BF),
        pltpu.VMEM((1, SLOTS), jnp.int32),
        pltpu.VMEM((2, 1, SLOTS), F32),
        pltpu.VMEM((2, 4, SLOTS, QB), F32),
        pltpu.VMEM((2, 4, SLOTS, QB), BF),
        pltpu.VMEM((2, SLOTS, QB), BF),
        pltpu.VMEM((2, HD, SLOTS), BF),
        pltpu.VMEM((12, HD, BLK), BF),
        pltpu.VMEM((2, BLK, 384), BF),
        pltpu.VMEM((BLK, FEAT), F32),
        pltpu.VMEM((BLK, FEAT), BF),
        pltpu.VMEM((BLK, FEAT), BF),
        pltpu.VMEM((2, 2, HD, SLOTS), F32),
        pltpu.VMEM((2, HD, 512), F32),
        pltpu.VMEM((2, 3, HD, SLOTS), BF),
        pltpu.VMEM((2, HD, 512), BF),
        pltpu.VMEM((12, 3, HD, BLK), BF),
        pltpu.VMEM((FEAT, BLK), F32),
        pltpu.VMEM((3, 2, HD, 512), BF),
        pltpu.VMEM((8, 3, 96, BLK), F32),
        pltpu.VMEM((8, 3, 96, BLK), BF),
        pltpu.VMEM((7, 3, 96, BLK), BF),
        pltpu.VMEM((8, 3, 16, BLK), F32),
        pltpu.VMEM((8, 3, 16, BLK), F32),
    ] + [
        dma(n)
        for n in (
            11, 3, 8, 8, 11, 3, 8, 8, 1, 1, (2, 3), (2, 4),
            (2, 8), 12, (3, 3), (3, 4), 1, 1, 1, 1, 8, 4, 4, 12, 12,
            7, 7, 8, 8,
        )
    ]
    proj, dq, dk, dv, dw = pl.pallas_call(
        kernel,
        out_shape=(rows, rows, rows, rows, jax.ShapeDtypeStruct((12, FEAT), BF)),
        in_specs=[hbm] * 5 + [smem],
        out_specs=[pl.BlockSpec(memory_space=pltpu.HBM)] * 4 + [vmem],
        scratch_shapes=scratch,
        compiler_params=pltpu.CompilerParams(
            collective_id=0, has_side_effects=True, vmem_limit_bytes=56 * 1024 * 1024
        ),
    )(queries, keys, values, w_out, grad_proj, frame_levels)
    strict = pl.BlockSpec(memory_space=pltpu.HBM)
    proj, dq, dk, dv, dw = pl.pallas_call(
        place,
        out_shape=(rows,) * 4 + (jax.ShapeDtypeStruct((12, FEAT), BF),),
        in_specs=[vmem] * 5,
        out_specs=[vmem] * 5,
        scratch_shapes=[],
    )(proj, dq, dk, dv, dw)
    return proj, dq, dk, dv, dw.T


def solution(mesh):
    rows = P("frame", "head")
    return jax.shard_map(
        local,
        mesh=mesh,
        in_specs=(rows, rows, rows, P("head", None), rows, P()),
        out_specs=(rows, rows, rows, rows, P("head", "frame")),
        check_vma=False,
    )
```

time: 56.5 us -> 55.5 us (0.982); the launches traced: 56.3 us -> 54.6 us
  Pallas kernels: 55.7 us -> 53.9 us
    pallas_call x1, Pallas kernels: 53.6 us -> 51.8 us  [local(): pl.pallas_call(kernel, out_shape=(rows, rows, rows, rows, jax.ShapeDtypeS...]
where the time goes in v3:
time: 55.5 us; the launch traced here: 54.6 us
  Pallas kernels  53.9 us (97%)
  between operations  0.64 us (1%)
    pallas_call x1, Pallas kernels, local(): pl.pallas_call(kernel, out_shape=(rows, rows, rows, rows, jax.ShapeDtypeS...  51.8 us
    pallas_call x1, Pallas kernels, local(): pl.pallas_call(place, out_shape=(rows,) * 4 + (jax.ShapeDtypeStruct((12,...  2.11 us

profile of v3, /device:TPU:1, one launch (start us, length us, event | category | flops | bytes accessed | tf_op | source)
XLA Modules:
  0.0 54.6 jit_solution(15227841169259965626)
XLA Ops:
  0.6 51.8 %shard_map.101 = (bf16[128,768]{1,0:T(8,128)(2,1)}, bf16[128,768]{1,0:T(8,128)(2,1)}, bf16[128,768]{1,0:T(8,128)(2,1)}, bf16[128,768]{1,0:T(8,128)(2,1)}, bf16[12,768]{1,0:T(8,128)(2,1)}) custom-call(bf16[128,768]{1,0:T(8,128)(2,1)} %q_hbm.1, bf16[128,768]{1,0:T(8,128)(2,1)} %k_hbm.1, bf16[128,768]{1,0:T(8,128)(2,1)} %v_hbm.1, bf16[768,1536]{1,0:T(8,128)(2,1)} %w_hbm.1, ...), custom_call_target="tpu_custom_call" | custom-call | tf_op jit(solution)/shard_map/pallas_call | solution.py:571
  52.5 2.1 %shard_map.102 = (bf16[128,768]{1,0:T(8,128)(2,1)}, bf16[128,768]{1,0:T(8,128)(2,1)}, bf16[128,768]{1,0:T(8,128)(2,1)}, bf16[128,768]{1,0:T(8,128)(2,1)}, bf16[12,768]{1,0:T(8,128)(2,1)}) custom-call(bf16[128,768]{1,0:T(8,128)(2,1)} %get-tuple-element.15.refs_0_, bf16[128,768]{1,0:T(8,128)(2,1)} %get-tuple-element.16.refs_1_, ...), custom_call_target="tpu_custom_call" | custom-call | tf_op jit(solution)/shard_map/pallas_call | solution.py:582

commit v4 on v3

--- a/solution.py
+++ b/solution.py
@@ -184,7 +184,7 @@
     loads[4].wait()
     for t in range(3):
         dpart[t * QB:(t + 1) * QB, :] = mm(w_ref[t * QB:(t + 1) * QB, own_cols], g_ref[...], 1, 1)
-    for copy in x_remote:
+    for copy in x_remote[:7]:
         copy.wait_send()
     gsend = rcopy(g_ref, gfull.at[:, own_cols], s_g.at[0], r_g.at[0], me, 1 - hd)
     gsend.start()
@@ -493,7 +493,7 @@
         copy.wait()
 
     gsend.wait_send()
-    for copy in d_remote + shared_plan(rx, s_xf, r_xc) + shared_plan(rd, s_df, r_dc) + gy_near[:2] + gy_far[:2] + gy_far_fwd + ay_remote + f_remote:
+    for copy in x_remote[7:] + d_remote + shared_plan(rx, s_xf, r_xc) + shared_plan(rd, s_df, r_dc) + gy_near[:2] + gy_far[:2] + gy_far_fwd + ay_remote + f_remote:
         copy.wait_send()
     xc_copy.wait_send()
     p_copy.wait_send()
@@ -515,8 +515,16 @@
 
 
 def place(*refs):
-    for i in range(5):
-        refs[5 + i][...] = refs[i][...]
+    sems = refs[15]
+    loads = [pltpu.make_async_copy(refs[i], refs[10 + i], sems.at[i]) for i in range(5)]
+    stores = [pltpu.make_async_copy(refs[10 + i], refs[5 + i], sems.at[5 + i]) for i in range(5)]
+    for copy in loads:
+        copy.start()
+    for load, store in zip(loads, stores):
+        load.wait()
+        store.start()
+    for copy in stores:
+        copy.wait()
 
 
 def local(queries, keys, values, w_out, grad_proj, frame_levels):
@@ -582,9 +590,9 @@
     proj, dq, dk, dv, dw = pl.pallas_call(
         place,
         out_shape=(rows,) * 4 + (jax.ShapeDtypeStruct((12, FEAT), BF),),
-        in_specs=[vmem] * 5,
-        out_specs=[vmem] * 5,
-        scratch_shapes=[],
+        in_specs=[strict] * 5,
+        out_specs=[strict] * 5,
+        scratch_shapes=[pltpu.VMEM((BLK, FEAT), BF)] * 4 + [pltpu.VMEM((12, FEAT), BF), dma(10)],
     )(proj, dq, dk, dv, dw)
     return proj, dq, dk, dv, dw.T
 

time: 55.5 us -> 54.7 us (0.986)
  no operation moved by 1% of the time
where the time goes in v4:
time: 54.7 us; the launch traced here: 54.2 us
  Pallas kernels  53.6 us (98%)
  between operations  0.64 us (1%)
    pallas_call x1, Pallas kernels, local(): pl.pallas_call(kernel, out_shape=(rows, rows, rows, rows, jax.ShapeDtypeS...  51.6 us
    pallas_call x1, Pallas kernels, local(): pl.pallas_call(place, out_shape=(rows,) * 4 + (jax.ShapeDtypeStruct((12,...  1.99 us

profile of v4, /device:TPU:1, one launch (start us, length us, event | category | flops | bytes accessed | tf_op | source)
XLA Modules:
  0.0 54.2 jit_solution(4113682159226720003)
XLA Ops:
  0.6 51.6 %shard_map.101 = (bf16[128,768]{1,0:T(8,128)(2,1)}, bf16[128,768]{1,0:T(8,128)(2,1)}, bf16[128,768]{1,0:T(8,128)(2,1)}, bf16[128,768]{1,0:T(8,128)(2,1)}, bf16[12,768]{1,0:T(8,128)(2,1)}) custom-call(bf16[128,768]{1,0:T(8,128)(2,1)} %q_hbm.1, bf16[128,768]{1,0:T(8,128)(2,1)} %k_hbm.1, bf16[128,768]{1,0:T(8,128)(2,1)} %v_hbm.1, bf16[768,1536]{1,0:T(8,128)(2,1)} %w_hbm.1, ...), custom_call_target="tpu_custom_call" | custom-call | tf_op jit(solution)/shard_map/pallas_call | solution.py:579
  52.2 2.0 %shard_map.102 = (bf16[128,768]{1,0:T(8,128)(2,1)}, bf16[128,768]{1,0:T(8,128)(2,1)}, bf16[128,768]{1,0:T(8,128)(2,1)}, bf16[128,768]{1,0:T(8,128)(2,1)}, bf16[12,768]{1,0:T(8,128)(2,1)}) custom-call(bf16[128,768]{1,0:T(8,128)(2,1)} %get-tuple-element.15.refs_0_, bf16[128,768]{1,0:T(8,128)(2,1)} %get-tuple-element.16.refs_1_, ...), custom_call_target="tpu_custom_call" | custom-call | tf_op jit(solution)/shard_map/pallas_call | solution.py:590

commit v5 on v4

--- a/solution.py
+++ b/solution.py
@@ -416,6 +416,10 @@
 
     attended_part(0)
     gsend.wait_recv()
+    transposed_half(1 - hd)
+    gy_far = gy_plan(1 - hd, 1)
+    for copy in gy_far:
+        copy.start()
     other_cols = pl.ds(pl.multiple_of((1 - hd) * FEAT, BLK), FEAT)
     for t in range(3):
         rows = slice(t * QB, (t + 1) * QB)
@@ -427,10 +431,6 @@
         copy.start()
     attended_part(1)
     attended_part(2)
-    transposed_half(1 - hd)
-    gy_far = gy_plan(1 - hd, 1)
-    for copy in gy_far:
-        copy.start()
     gy_far_fwd = gy_forward(hd, 0)
     forward_shared(dat, rd, s_df, r_dc)
     gy_arrived(hd, 0)

time: 54.7 us -> 54.9 us (level)
    pallas_call x1, Pallas kernels: 51.6 us -> 52.2 us  [local(): pl.pallas_call(kernel, out_shape=(rows, rows, rows, rows, jax.ShapeDtypeS...]
where the time goes in v5:
time: 54.9 us; the launch traced here: 54.8 us
  Pallas kernels  54.1 us (99%)
  between operations  0.64 us (1%)
    pallas_call x1, Pallas kernels, local(): pl.pallas_call(kernel, out_shape=(rows, rows, rows, rows, jax.ShapeDtypeS...  52.2 us
    pallas_call x1, Pallas kernels, local(): pl.pallas_call(place, out_shape=(rows,) * 4 + (jax.ShapeDtypeStruct((12,...  1.99 us

profile of v5, /device:TPU:1, one launch (start us, length us, event | category | flops | bytes accessed | tf_op | source)
XLA Modules:
  0.0 54.8 jit_solution(18314998957727420049)
XLA Ops:
  0.6 52.2 %shard_map.101 = (bf16[128,768]{1,0:T(8,128)(2,1)}, bf16[128,768]{1,0:T(8,128)(2,1)}, bf16[128,768]{1,0:T(8,128)(2,1)}, bf16[128,768]{1,0:T(8,128)(2,1)}, bf16[12,768]{1,0:T(8,128)(2,1)}) custom-call(bf16[128,768]{1,0:T(8,128)(2,1)} %q_hbm.1, bf16[128,768]{1,0:T(8,128)(2,1)} %k_hbm.1, bf16[128,768]{1,0:T(8,128)(2,1)} %v_hbm.1, bf16[768,1536]{1,0:T(8,128)(2,1)} %w_hbm.1, ...), custom_call_target="tpu_custom_call" | custom-call | tf_op jit(solution)/shard_map/pallas_call | solution.py:579
  52.8 2.0 %shard_map.102 = (bf16[128,768]{1,0:T(8,128)(2,1)}, bf16[128,768]{1,0:T(8,128)(2,1)}, bf16[128,768]{1,0:T(8,128)(2,1)}, bf16[128,768]{1,0:T(8,128)(2,1)}, bf16[12,768]{1,0:T(8,128)(2,1)}) custom-call(bf16[128,768]{1,0:T(8,128)(2,1)} %get-tuple-element.15.refs_0_, bf16[128,768]{1,0:T(8,128)(2,1)} %get-tuple-element.16.refs_1_, ...), custom_call_target="tpu_custom_call" | custom-call | tf_op jit(solution)/shard_map/pallas_call | solution.py:590
